TPU v7x, 32 devices: a whole 2x2x4 slice. The times are simulated.
32 devices in a mesh: wide: 16 (over z, y, x), rep: 2 (over core).
Axes of the slice: x: 2, y: 2, z: 4, core: 2. Of those that a mesh axis runs over, the one named last changes fastest.
Arguments:
- images: bfloat16 [64, 256, 512], P('rep', 'wide'), may hold values from -6 to 6
- cotangent: bfloat16 [64, 256, 512], P('rep', 'wide'), may hold values from -6 to 6
- levels: int32 [64], P('rep'), may hold values from 0 to 1999
- noise_table: bfloat16 [2000, 512], replicated, may hold values from -6 to 6
- gain_one: float32 [512], replicated, may hold values from 0.1 to 1.9
- shift_one: float32 [512], replicated, may hold values from -3 to 3
- conv_one: bfloat16 [4608, 512], replicated, may hold values from -0.09375 to 0.09375
- bias_one: float32 [512], replicated, may hold values from -3 to 3
- embed_weight: bfloat16 [512, 512], replicated, may hold values from -0.25 to 0.25
- embed_bias: float32 [512], replicated, may hold values from -3 to 3
- gain_two: float32 [512], replicated, may hold values from 0.1 to 1.9
- shift_two: float32 [512], replicated, may hold values from -3 to 3
- conv_two: bfloat16 [4608, 512], replicated, may hold values from -0.09375 to 0.09375
- bias_two: float32 [512], replicated, may hold values from -3 to 3
- gain_three: float32 [512], replicated, may hold values from 0.1 to 1.9
- shift_three: float32 [512], replicated, may hold values from -3 to 3
- query_weight: bfloat16 [512, 512], replicated, may hold values from -0.25 to 0.25
- query_bias: float32 [512], replicated, may hold values from -3 to 3
- key_weight: bfloat16 [512, 512], replicated, may hold values from -0.25 to 0.25
- value_weight: bfloat16 [512, 512], replicated, may hold values from -0.25 to 0.25
- value_bias: float32 [512], replicated, may hold values from -3 to 3
- out_weight: bfloat16 [512, 512], replicated, may hold values from -2 to 2
- out_bias: float32 [512], replicated, may hold values from -3 to 3
Outputs:
- output: bfloat16 [64, 256, 512], P('rep', 'wide')
- input_grad: bfloat16 [64, 256, 512], P('rep', 'wide')
- table_grad: float32 [1024000], P(('wide', 'rep'))
- conv_one_grad: float32 [2359296], P(('wide', 'rep'))
- conv_two_grad: float32 [2359296], P(('wide', 'rep'))
- embed_weight_grad: float32 [262144], P(('wide', 'rep'))
- query_weight_grad: float32 [262144], P(('wide', 'rep'))
- key_weight_grad: float32 [262144], P(('wide', 'rep'))
- value_weight_grad: float32 [262144], P(('wide', 'rep'))
- out_weight_grad: float32 [262144], P(('wide', 'rep'))
- gain_one_grad: float32 [512], replicated
- shift_one_grad: float32 [512], replicated
- bias_one_grad: float32 [512], replicated
- embed_bias_grad: float32 [512], replicated
- gain_two_grad: float32 [512], replicated
- shift_two_grad: float32 [512], replicated
- bias_two_grad: float32 [512], replicated
- gain_three_grad: float32 [512], replicated
- shift_three_grad: float32 [512], replicated
- query_bias_grad: float32 [512], replicated
- value_bias_grad: float32 [512], replicated
- out_bias_grad: float32 [512], replicated
All inputs are finite; a program needn't handle non-finite values.
Results may differ from a plain program's by a relative error of at most 0.015.
Values may be sent and summed in bfloat16 or wider, within the bound.
A program may use at most 192 MiB of HBM per device.

v0:
```python
import jax
import jax.numpy as jnp
from jax import lax
from jax.sharding import PartitionSpec as P

GROUPS = 32
SIDE = 16


epsilon = 1e-05
highest = lax.Precision.HIGHEST


def swish(field):
    return field * jax.nn.sigmoid(field)


def group_norm(field, norm_gain, norm_shift):
    images_here = field.shape[0]
    channels = field.shape[2]
    grouped = field.reshape(images_here, field.shape[1], GROUPS, channels // GROUPS)
    center = jnp.mean(grouped, axis=(1, 3), keepdims=True)
    spread = grouped - center
    variance = jnp.mean(spread * spread, axis=(1, 3), keepdims=True)
    return (spread * lax.rsqrt(variance + epsilon)).reshape(field.shape) * norm_gain + norm_shift


def norm_swish(field, norm_gain, norm_shift):
    return swish(group_norm(field, norm_gain, norm_shift))


def matmul(left, right):
    return jnp.dot(left, right, preferred_element_type=jnp.float32)


def contract_rows(left, right):
    return lax.dot_general(
        left, right, (((0,), (0,)), ((), ())), preferred_element_type=jnp.float32
    )


def against(left, right):
    return lax.dot_general(
        left, right, (((1,), (1,)), ((), ())), preferred_element_type=jnp.float32
    )


def patches(activation):
    images_here = activation.shape[0]
    grid = activation.reshape(images_here, SIDE, SIDE, activation.shape[2])
    padded = jnp.pad(grid, ((0, 0), (1, 1), (1, 1), (0, 0)))
    pieces = [
        padded[
            :, kernel_tap // 3 : kernel_tap // 3 + SIDE, kernel_tap % 3 : kernel_tap % 3 + SIDE, :
        ]
        for kernel_tap in range(9)
    ]
    return jnp.concatenate(pieces, axis=-1).reshape(images_here * SIDE * SIDE, -1)


def unpatch(columns, images_here):
    channels = columns.shape[1] // 9
    grid = columns.reshape(images_here, SIDE, SIDE, 9, channels)
    summed = jnp.zeros((images_here, SIDE + 2, SIDE + 2, channels), jnp.float32)
    for kernel_tap in range(9):
        row_off = kernel_tap // 3
        col_off = kernel_tap % 3
        summed = summed + jnp.pad(
            grid[:, :, :, kernel_tap, :],
            ((0, 0), (row_off, 2 - row_off), (col_off, 2 - col_off), (0, 0)),
        )
    return summed[:, 1 : SIDE + 1, 1 : SIDE + 1, :].reshape(images_here, SIDE * SIDE, channels)


def per_device(
    images,
    cotangent,
    levels,
    noise_table,
    gain_one,
    shift_one,
    conv_one,
    bias_one,
    embed_weight,
    embed_bias,
    gain_two,
    shift_two,
    conv_two,
    bias_two,
    gain_three,
    shift_three,
    query_weight,
    query_bias,
    key_weight,
    value_weight,
    value_bias,
    out_weight,
    out_bias,
):
    arrived, upstream = (
        lax.all_to_all(images, "wide", split_axis=0, concat_axis=1, tiled=True),
        lax.all_to_all(cotangent, "wide", split_axis=0, concat_axis=1, tiled=True),
    )
    images_here = arrived.shape[0]
    pixels = arrived.shape[1]
    channels = arrived.shape[2]
    flat_rows = images_here * pixels
    score_scale = channels ** (-0.5)
    table_rows = noise_table.shape[0]
    offset = lax.axis_index("wide") * images_here
    own_levels = lax.dynamic_slice_in_dim(levels, offset, images_here)
    selector = own_levels[:, None] == jnp.arange(table_rows, dtype=jnp.int32)[None, :]
    embedded = matmul(selector.astype(jnp.bfloat16), noise_table).astype(jnp.bfloat16)
    embed_shift = matmul(embedded, embed_weight) + embed_bias
    inputs = arrived.astype(jnp.float32)
    act_one, back_one = jax.vjp(norm_swish, inputs, gain_one, shift_one)
    cols_one = patches(act_one.astype(jnp.bfloat16))
    hidden_one = (matmul(cols_one, conv_one) + bias_one).reshape(images_here, pixels, channels)
    hidden_one = hidden_one + embed_shift[:, None, :]
    act_two, back_two = jax.vjp(norm_swish, hidden_one, gain_two, shift_two)
    cols_two = patches(act_two.astype(jnp.bfloat16))
    branch_out = matmul(cols_two, conv_two) + bias_two
    middle = inputs + branch_out.reshape(images_here, pixels, channels)
    normed, back_three = jax.vjp(group_norm, middle, gain_three, shift_three)
    normed_low = normed.astype(jnp.bfloat16).reshape(flat_rows, channels)
    query_block = (matmul(normed_low, query_weight) + query_bias).astype(jnp.bfloat16)
    key_block = matmul(normed_low, key_weight).astype(jnp.bfloat16)
    value_block = (matmul(normed_low, value_weight) + value_bias).astype(jnp.bfloat16)
    query_block = query_block.reshape(images_here, pixels, channels)
    key_block = key_block.reshape(images_here, pixels, channels)
    value_block = value_block.reshape(images_here, pixels, channels)
    scores = (
        jnp.einsum("npc,nqc->npq", query_block, key_block, preferred_element_type=jnp.float32)
        * score_scale
    )
    row_top = jnp.max(scores, axis=-1, keepdims=True)
    exponent = jnp.exp(scores - row_top)
    row_total = jnp.sum(exponent, axis=-1, keepdims=True)
    probs_low = (exponent / row_total).astype(jnp.bfloat16)
    log_total = row_top + jnp.log(row_total)
    mixed = jnp.einsum("npq,nqc->npc", probs_low, value_block, preferred_element_type=jnp.float32)
    mixed_low = mixed.astype(jnp.bfloat16).reshape(flat_rows, channels)
    result = middle.reshape(flat_rows, channels) + matmul(mixed_low, out_weight) + out_bias
    grad_out = upstream.reshape(flat_rows, channels)
    grad_out_bias = jnp.sum(grad_out.astype(jnp.float32), axis=0)
    grad_out_weight = contract_rows(mixed_low, grad_out)
    grad_mixed = (
        against(grad_out, out_weight).astype(jnp.bfloat16).reshape(images_here, pixels, channels)
    )
    scores_again = (
        jnp.einsum("npc,nqc->npq", query_block, key_block, preferred_element_type=jnp.float32)
        * score_scale
    )
    probs = jnp.exp(scores_again - log_total)
    probs_again = probs.astype(jnp.bfloat16)
    grad_probs = jnp.einsum(
        "npc,nqc->npq", grad_mixed, value_block, preferred_element_type=jnp.float32
    )
    grad_values = jnp.einsum(
        "npq,npc->nqc", probs_again, grad_mixed, preferred_element_type=jnp.float32
    ).astype(jnp.bfloat16)
    grad_scores = probs * (grad_probs - jnp.sum(grad_probs * probs, axis=-1, keepdims=True))
    grad_scores = grad_scores.astype(jnp.bfloat16)
    grad_query = (
        (
            jnp.einsum("npq,nqc->npc", grad_scores, key_block, preferred_element_type=jnp.float32)
            * score_scale
        )
        .astype(jnp.bfloat16)
        .reshape(flat_rows, channels)
    )
    grad_keys = (
        (
            jnp.einsum("npq,npc->nqc", grad_scores, query_block, preferred_element_type=jnp.float32)
            * score_scale
        )
        .astype(jnp.bfloat16)
        .reshape(flat_rows, channels)
    )
    grad_values = grad_values.reshape(flat_rows, channels)
    grad_query_weight = contract_rows(normed_low, grad_query)
    grad_key_weight = contract_rows(normed_low, grad_keys)
    grad_value_weight = contract_rows(normed_low, grad_values)
    grad_query_bias = jnp.sum(grad_query.astype(jnp.float32), axis=0)
    grad_value_bias = jnp.sum(grad_values.astype(jnp.float32), axis=0)
    grad_normed = against(grad_query, query_weight) + against(grad_keys, key_weight)
    grad_normed = grad_normed + against(grad_values, value_weight)
    grad_middle, grad_gain_three, grad_shift_three = back_three(
        grad_normed.reshape(images_here, pixels, channels)
    )
    grad_middle = grad_middle + upstream.astype(jnp.float32)
    grad_branch = grad_middle.astype(jnp.bfloat16).reshape(flat_rows, channels)
    grad_bias_two = jnp.sum(grad_branch.astype(jnp.float32), axis=0)
    grad_conv_two = contract_rows(cols_two, grad_branch)
    grad_act_two = unpatch(against(grad_branch, conv_two), images_here)
    grad_hidden, grad_gain_two, grad_shift_two = back_two(grad_act_two)
    grad_hidden_low = grad_hidden.astype(jnp.bfloat16)
    hidden_rows = grad_hidden_low.reshape(flat_rows, channels)
    grad_bias_one = jnp.sum(hidden_rows.astype(jnp.float32), axis=0)
    grad_conv_one = contract_rows(cols_one, hidden_rows)
    grad_shift = jnp.sum(grad_hidden_low.astype(jnp.float32), axis=1)
    grad_embed_bias = jnp.sum(grad_shift, axis=0)
    grad_embed_weight = jnp.dot(embedded.astype(jnp.float32).T, grad_shift, precision=highest)
    embed_float = embed_weight.astype(jnp.float32)
    grad_act_one = unpatch(against(hidden_rows, conv_one), images_here)
    grad_input_part, grad_gain_one, grad_shift_one = back_one(grad_act_one)
    grad_input = grad_middle + grad_input_part
    output_back, input_back = (
        lax.all_to_all(
            result.reshape(images_here, pixels, channels).astype(jnp.bfloat16),
            "wide",
            split_axis=1,
            concat_axis=0,
            tiled=True,
        ),
        lax.all_to_all(
            grad_input.astype(jnp.bfloat16), "wide", split_axis=1, concat_axis=0, tiled=True
        ),
    )
    wide_count = lax.axis_size("wide")
    rep_count = lax.axis_size("rep")
    device_count = wide_count * rep_count
    weight_grads = (
        grad_conv_one,
        grad_conv_two,
        grad_embed_weight,
        grad_query_weight,
        grad_key_weight,
        grad_value_weight,
        grad_out_weight,
    )
    grad_embedded = jnp.dot(grad_shift, embed_float.T, precision=highest)
    grad_table = jnp.dot(selector.astype(jnp.float32).T, grad_embedded, precision=highest)
    members = (grad_table,) + weight_grads
    widths = [member.size // device_count for member in members]
    packed = jnp.concatenate([member.reshape(device_count, -1) for member in members], axis=1)
    packed = lax.psum_scatter(packed, ("wide", "rep"), scatter_dimension=0, tiled=True)
    packed = packed.reshape(-1)
    large_grads = []
    start_at = 0
    for width in widths:
        large_grads.append(packed[start_at : start_at + width])
        start_at = start_at + width
    large_grads = tuple(large_grads)
    small_grads = lax.psum(
        (
            grad_gain_one,
            grad_shift_one,
            grad_bias_one,
            grad_embed_bias,
            grad_gain_two,
            grad_shift_two,
            grad_bias_two,
            grad_gain_three,
            grad_shift_three,
            grad_query_bias,
            grad_value_bias,
            grad_out_bias,
        ),
        ("wide", "rep"),
    )
    return (output_back, input_back) + large_grads + tuple(small_grads)


def solution(mesh):
    in_specs = (
        P("rep", "wide", None),
        P("rep", "wide", None),
        P("rep"),
        P(),
        P(),
        P(),
        P(),
        P(),
        P(),
        P(),
        P(),
        P(),
        P(),
        P(),
        P(),
        P(),
        P(),
        P(),
        P(),
        P(),
        P(),
        P(),
        P(),
    )
    out_specs = (
        P("rep", "wide", None),
        P("rep", "wide", None),
        P(("wide", "rep")),
        P(("wide", "rep")),
        P(("wide", "rep")),
        P(("wide", "rep")),
        P(("wide", "rep")),
        P(("wide", "rep")),
        P(("wide", "rep")),
        P(("wide", "rep")),
        P(),
        P(),
        P(),
        P(),
        P(),
        P(),
        P(),
        P(),
        P(),
        P(),
        P(),
        P(),
    )
    return jax.shard_map(
        per_device, mesh=mesh, in_specs=in_specs, out_specs=out_specs, check_vma=False
    )
```

profile of v0, /device:TPU:0, one launch (start us, length us, event | category | flops | bytes accessed | tf_op | source)
XLA Modules:
  0.0 731.7 jit_solution(4899452459404374509)
XLA Ops:
  7.2 8.5 %all-to-all-start = ((bf16[32,16,512]{2,1,0:T(8,128)(2,1)}), bf16[32,16,512]{2,1,0:T(8,128)(2,1)S(1)}, u32[]{:S(2)}, u32[]{:S(2)}) async-start(bf16[32,16,512]{2,1,0:T(8,128)(2,1)} %param.23), calls=%async_computation | async-start | bytes 1048576 | tf_op jit(solution)/shard_map/all_to_all | solution.py:101
  20.4 10.4 %all-to-all-done = bf16[32,16,512]{2,1,0:T(8,128)(2,1)S(1)} async-done(((bf16[32,16,512]{2,1,0:T(8,128)(2,1)}), bf16[32,16,512]{2,1,0:T(8,128)(2,1)S(1)}, u32[]{:S(2)}, u32[]{:S(2)}) %all-to-all-start) | async-done | bytes 524320 | tf_op jit(solution)/shard_map/all_to_all | solution.py:101
  30.8 4.2 all-to-all-start.2
  35.3 4.9 reshape.496
  64.7 3.6 convolution_add_fusion.5
  68.3 6.6 reshape.510
  74.9 11.2 %fusion.55 = (f32[2,32]{1,0:T(2,128)S(1)}, f32[2,256,32,16]{3,2,1,0:T(8,128)}) fusion(f32[2,256,32,16]{3,2,1,0:T(8,128)} %reshape.496, f32[2,256,32,16]{3,2,1,0:T(8,128)} %reshape.510), kind=kLoop, calls=%fused_computation.225 | loop fusion | flops 524224 | bytes 3145984 | tf_op jit(solution)/shard_map/jvp()/reduce_sum | solution.py:22
  86.1 4.8 multiply_reduce_fusion.1
  108.4 6.2 reshape.511
  114.5 8.1 %multiply_reduce_fusion = f32[2,32]{1,0:T(2,128)S(1)} fusion(f32[2,256,32,16]{3,2,1,0:T(8,128)} %reshape.511, f32[2,256,32,16]{3,2,1,0:T(8,128)} %get-tuple-element.55, f32[32,16]{1,0:T(8,128)S(1)} %mul.493, f32[2,32]{1,0:T(2,128)S(1)} %broadcast_multiply_fusion), kind=kLoop, calls=%fused_computation.2 | loop fusion | flops 1048512 | bytes 2099712 | tf_op jit(solution)/shard_map/transpose(jvp())/reduce_sum | solution.py:25
  122.7 4.9 fusion
  130.2 7.7 %fusion.64 = f32[4608,512]{1,0:T(8,128)} fusion(bf16[512,4608]{1,0:T(8,128)(2,1)} %copy-done.7, bf16[512,512]{1,0:T(8,128)(2,1)S(1)} %get-tuple-element.85), kind=kOutput, calls=%fused_computation.235 | convolution fusion | flops 2415919104 | bytes 14680064 | tf_op jit(solution)/shard_map/dot_general | solution.py:37
  140.5 3.1 slice_bitcast_fusion.17
  147.9 6.2 reshape.485
  154.1 7.2 copy.283
  169.3 7.8 %fusion.63 = f32[4608,512]{1,0:T(8,128)} fusion(bf16[512,4608]{1,0:T(8,128)(2,1)} %copy-done.6, bf16[512,512]{1,0:T(8,128)(2,1)S(1)} %get-tuple-element.46), kind=kOutput, calls=%fused_computation.234 | convolution fusion | flops 2415919104 | bytes 14680064 | tf_op jit(solution)/shard_map/dot_general | solution.py:37
  177.0 4.7 fusion.61
  181.8 3.1 slice_bitcast_fusion.8
  197.1 3.6 add_convert_fusion
  204.1 3.8 fusion.43
  207.9 5.2 reshape.487
  213.1 4.4 constant_dynamic-update-slice_fusion.25
  217.6 8.1 %reshape.488 = f32[32,73728]{1,0:T(8,128)} reshape(f32[4608,512]{1,0:T(8,128)} %fusion.63) | data formatting | bytes 18874368 | tf_op jit(solution)/shard_map/reshape | solution.py:236
  225.6 8.2 %reshape.489 = f32[32,73728]{1,0:T(8,128)} reshape(f32[4608,512]{1,0:T(8,128)} %fusion.64) | data formatting | bytes 18874368 | tf_op jit(solution)/shard_map/reshape | solution.py:236
  245.0 8.4 %constant_dynamic-update-slice_fusion.24 = f32[32,220416]{1,0:T(8,128)} fusion(f32[32,220416]{1,0:T(8,128)} %constant_dynamic-update-slice_fusion.25, f32[32,73728]{1,0:T(8,128)} %reshape.488), kind=kLoop, calls=%fused_computation.197 | loop fusion | bytes 18874368
  253.4 4.2 constant_dynamic-update-slice_fusion.23
  266.3 6.8 all-to-all-start.1
  274.4 20.8 %all-to-all-done.1 = bf16[2,256,512]{2,0,1:T(2,128)(2,1)S(1)} async-done(((bf16[2,256,512]{2,0,1:T(2,128)(2,1)}), bf16[2,256,512]{2,0,1:T(2,128)(2,1)S(1)}, u32[]{:S(2)}, u32[]{:S(2)}) %all-to-all-start.1) | async-done | bytes 524320 | tf_op jit(solution)/shard_map/all_to_all | solution.py:209
  295.3 3.6 all-to-all-start.3
  300.0 42.8 %all-reduce.21 = (f32[512]{0:T(512)}, f32[512]{0:T(512)}, f32[512]{0:T(512)}, f32[512]{0:T(512)}, f32[512]{0:T(512)}, /*index=5*/f32[512]{0:T(512)}, f32[512]{0:...) all-reduce(f32[512]{0:T(512)S(1)} %get-tuple-element.112, ...), channel_id=1, replica_groups=mesh['wide'=16,'rep'=2] {'wide','rep'}, use_global_device_ids=true, to_apply=%region_23.24 | all-reduce | flops 6144 | bytes 49152 | tf_op jit(solution)/shard_map/psum | solution.py:245
  344.6 370.8 %all-reduce.24.cloned.1.call-done = f32[32,220416]{1,0:T(8,128)} async-done(((f32[32,220416]{1,0:T(8,128)}), f32[32,220416]{1,0:T(8,128)}) %all-reduce.24.cloned.1.call-update) | async-done | bytes 28213264
  717.7 4.5 fusion.57
  (266 shorter events, 108.0 us)
Async XLA Ops:
  7.2 9.2 %copy-start = (bf16[2000,512]{1,0:T(8,128)(2,1)S(1)}, bf16[2000,512]{1,0:T(8,128)(2,1)}, u32[]{:S(2)}) copy-start(bf16[2000,512]{1,0:T(8,128)(2,1)} %param.26) | copy-start | bytes 6144004
  7.2 23.6 %all-to-all-start = ((bf16[32,16,512]{2,1,0:T(8,128)(2,1)}), bf16[32,16,512]{2,1,0:T(8,128)(2,1)S(1)}, u32[]{:S(2)}, u32[]{:S(2)}) async-start(bf16[32,16,512]{2,1,0:T(8,128)(2,1)} %param.23), calls=%async_computation | async-start | bytes 1048576 | tf_op jit(solution)/shard_map/all_to_all | solution.py:101
  30.8 69.5 %all-to-all-start.2 = ((bf16[32,16,512]{2,1,0:T(8,128)(2,1)}), bf16[32,16,512]{2,1,0:T(8,128)(2,1)}, u32[]{:S(2)}, u32[]{:S(2)}) async-start(bf16[32,16,512]{2,1,0:T(8,128)(2,1)} %param.24), calls=%async_computation.2 | async-start | bytes 1048576 | tf_op jit(solution)/shard_map/all_to_all | solution.py:102
  35.1 680.4 %all-reduce.24.cloned.1.call-start = ((), (), s32[]{:S(2)}) async-start(), calls=%async_computation.4 | async-start | bytes 56426496
  35.2 7.0 copy-start.41
  35.3 7.0 copy-start.43
  50.8 9.0 %copy-start.39 = (f32[512]{0:T(512)S(1)}, f32[512]{0:T(512)}, u32[]{:S(2)}) copy-start(f32[512]{0:T(512)} %param.34) | copy-start | bytes 6148
  50.8 9.0 %copy-start.40 = (f32[512]{0:T(512)S(1)}, f32[512]{0:T(512)}, u32[]{:S(2)}) copy-start(f32[512]{0:T(512)} %param.33) | copy-start | bytes 6148
  86.1 5.2 copy-start.5
  86.1 5.3 copy-start.42
  86.1 5.3 copy-start.44
  90.9 4.9 copy-start.48
  91.4 7.0 copy-start.9
  91.4 6.6 copy-start.36
  91.4 6.5 copy-start.49
  114.5 8.2 %copy-start.2 = (f32[2,256,32,16]{3,2,1,0:T(8,128)S(1)}, f32[2,256,32,16]{3,2,1,0:T(8,128)}, u32[]{:S(2)}) copy-start(f32[2,256,32,16]{3,2,1,0:T(8,128)} %reshape.511) | copy-start | bytes 3145732
  122.7 5.2 copy-start.11
  127.9 9.9 %slice-start.7 = ((s8[4718592]{0:T(1024)(128)(4,1)}), s8[4194304]{0:T(1024)(128)(4,1)S(1)}, s32[]{:S(2)}) async-start(s8[4718592]{0:T(1024)(128)(4,1)} %bitcast.354), calls=%async_computation.12 | async-start | bytes 8388608
  130.2 7.7 %slice-start.8 = ((s8[4718592]{0:T(1024)(128)(4,1)}), s8[524288]{0:T(1024)(128)(4,1)S(1)}, s32[]{:S(2)}) async-start(s8[4718592]{0:T(1024)(128)(4,1)} %bitcast.354), calls=%async_computation.13 | async-start | bytes 1048576
  189.7 7.4 %copy-start.3 = (f32[512,512]{1,0:T(8,128)S(1)}, f32[512,512]{1,0:T(8,128)}, u32[]{:S(2)}) copy-start(f32[512,512]{1,0:T(8,128)} %convolution_add_fusion) | copy-start | bytes 3145732
  192.1 5.0 copy-start.20
  195.7 5.0 copy-start.15
  197.1 5.5 copy-start.17
  225.6 8.2 %copy-start.21 = (f32[512,512]{1,0:T(8,128)S(1)}, f32[512,512]{1,0:T(8,128)}, u32[]{:S(2)}) copy-start(f32[512,512]{1,0:T(8,128)} %fusion.65) | copy-start | bytes 3145732
  242.5 10.9 %slice-start = ((s8[9437184]{0:T(1024)(128)(4,1)}), s8[1048576]{0:T(1024)(128)(4,1)S(1)}, s32[]{:S(2)}) async-start(s8[9437184]{0:T(1024)(128)(4,1)} %bitcast.342), calls=%async_computation.5 | async-start | bytes 2097152
  245.0 8.4 %slice-start.1 = ((s8[9437184]{0:T(1024)(128)(4,1)}), s8[4194304]{0:T(1024)(128)(4,1)S(1)}, s32[]{:S(2)}) async-start(s8[9437184]{0:T(1024)(128)(4,1)} %bitcast.342), calls=%async_computation.6 | async-start | bytes 8388608
  245.0 8.4 %slice-start.2 = ((s8[9437184]{0:T(1024)(128)(4,1)}), s8[4194304]{0:T(1024)(128)(4,1)S(1)}, s32[]{:S(2)}) async-start(s8[9437184]{0:T(1024)(128)(4,1)} %bitcast.342), calls=%async_computation.7 | async-start | bytes 8388608
  253.4 5.3 copy-start.24
  264.5 8.6 %copy-start.29 = (bf16[2,256,512]{2,1,0:T(8,128)(2,1)S(1)}, bf16[2,256,512]{2,1,0:T(8,128)(2,1)}, u32[]{:S(2)}) copy-start(bf16[2,256,512]{2,1,0:T(8,128)(2,1)} %get-tuple-element.83) | copy-start | bytes 1572868
  264.9 459.5 %copy-start.1 = (bf16[2000,512]{1,0:T(8,128)(2,1)S(1)}, bf16[2000,512]{1,0:T(8,128)(2,1)}, u32[]{:S(2)}) copy-start(bf16[2000,512]{1,0:T(8,128)(2,1)} %param.26) | copy-start | bytes 6144004
  266.3 29.0 %all-to-all-start.1 = ((bf16[2,256,512]{2,0,1:T(2,128)(2,1)}), bf16[2,256,512]{2,0,1:T(2,128)(2,1)S(1)}, u32[]{:S(2)}, u32[]{:S(2)}) async-start(bf16[2,256,512]{2,0,1:T(2,128)(2,1)} %copy.268), calls=%async_computation.1 | async-start | bytes 1048576 | tf_op jit(solution)/shard_map/all_to_all | solution.py:209
  295.3 48.5 %all-to-all-start.3 = ((bf16[2,256,512]{2,0,1:T(2,128)(2,1)}), bf16[2,256,512]{2,0,1:T(2,128)(2,1)S(1)}, u32[]{:S(2)}, u32[]{:S(2)}) async-start(bf16[2,256,512]{2,0,1:T(2,128)(2,1)} %copy.296), calls=%async_computation.3 | async-start | bytes 1048576 | tf_op jit(solution)/shard_map/all_to_all | solution.py:216
  (32 other events, 87.7 us)
Sparse Core Ops, SparseCore 0:
  263.1 452.2 all-reduce.23
where the time goes:
time: 741 us; the launch traced here: 732 us
  waiting for transfers between devices  402 us (54%)
  local copies, waits for them, and re-layouts  126 us (17%)
  other arithmetic  66.2 us (9%)
  matrix products  55.6 us (8%)
  blocking collectives  42.8 us (6%)
  starting transfers between devices  23.1 us (3%)
  between operations  15.5 us (2%)
    unnamed x2, waiting for transfers between devices  371 us
    psum x1, blocking collectives, per_device(): lax.psum((grad_gain_one, grad_shift_one, grad_bias_one, grad_embed_bias,...  42.8 us
    unnamed x140, local copies, waits for them, and re-layouts  32.2 us
    reshape x8, local copies, waits for them, and re-layouts, per_device(): member.reshape(device_count, -1)  30.2 us
    dot_general x6, matrix products, contract_rows(): lax.dot_general(left, right, (((0,), (0,)), ((), ())), preferred_element_...  21.3 us
    all_to_all x1, waiting for transfers between devices, per_device(): lax.all_to_all(result.reshape(images_here, pixels, channels).astype(jnp.b...  20.8 us
  transfers between devices with their start and end apart: 5, of which 3 were waited for; matrix products, arithmetic and copies ran while one was open for 9% of the time, Pallas kernels for 0%

commit v1 on v0

--- a/solution.py
+++ b/solution.py
@@ -1,10 +1,17 @@
+import functools
+import types
+
 import jax
 import jax.numpy as jnp
 from jax import lax
+from jax.experimental import pallas as pl
+from jax.experimental.pallas import tpu as pltpu
 from jax.sharding import PartitionSpec as P
 
 GROUPS = 32
 SIDE = 16
+MESH = pl.DeviceIdType.MESH
+CHUNK = 64
 
 
 epsilon = 1e-05
@@ -72,7 +79,7 @@
     return summed[:, 1 : SIDE + 1, 1 : SIDE + 1, :].reshape(images_here, SIDE * SIDE, channels)
 
 
-def per_device(
+def plain_device(
     images,
     cotangent,
     levels,
@@ -262,6 +269,1084 @@
     return (output_back, input_back) + large_grads + tuple(small_grads)
 
 
+def by_rows(left, right):
+    return lax.dot_general(
+        left, right, (((0,), (0,)), ((), ())), preferred_element_type=jnp.float32
+    )
+
+
+def group_sum(rows):
+    channels = rows.shape[1]
+    lane = lax.broadcasted_iota(jnp.int32, rows.shape, 1)
+    reach = 1
+    while reach < channels // GROUPS:
+        odd = (lane // reach) % 2
+        rows = rows + jnp.where(
+            odd == 0, pltpu.roll(rows, channels - reach, 1), pltpu.roll(rows, reach, 1)
+        )
+        reach = reach * 2
+    return rows
+
+
+def stack_rows(members):
+    shape = (8, members[0].shape[1])
+    place = lax.broadcasted_iota(jnp.int32, shape, 0)
+    stacked = jnp.zeros(shape, jnp.float32)
+    for index, member in enumerate(members):
+        stacked = jnp.where(place == index, jnp.broadcast_to(member, shape), stacked)
+    return stacked
+
+
+def sigmoid(field):
+    return 0.5 + 0.5 * jnp.tanh(0.5 * field)
+
+
+INPUTS = ("images", "cotangent", "noise_table", "conv_one", "conv_two", "embed_weight", "query_weight", "key_weight", "value_weight", "out_weight", "levels", "gain_one", "shift_one", "bias_one", "embed_bias", "gain_two", "shift_two", "bias_two", "gain_three", "shift_three", "query_bias", "value_bias", "out_bias")
+SUMS = ("gain_one", "shift_one", "bias_one", "gain_two", "shift_two", "bias_two", "gain_three", "shift_three", "query_bias", "value_bias", "out_bias")
+
+
+class Reduce:
+    def __init__(self, place, blocks, bits, landing, kept, send, recv, parts, last):
+        self.place, self.blocks, self.bits, self.last = place, blocks, bits, last
+        self.landing, self.kept, self.send, self.recv = landing, kept, send, recv
+        self.rows = blocks.shape[2]
+        self.parts = parts
+
+    def cut(self, part):
+        size = self.rows // self.parts
+        return pl.ds(part * size, size)
+
+    def copy(self, stage, part):
+        place, rows = self.place, self.cut(part)
+        if stage == 0:
+            source = self.blocks.at[:, 1 - place.core, rows, :]
+            target = place.other_core
+        else:
+            count = self.blocks.shape[0] >> stage
+            bit = self.bits[stage - 1]
+            source = self.kept[stage - 1].at[
+                pl.ds((1 - place.bit(bit)) * count, count), rows, :
+            ]
+            target = place.across(bit)
+        return pltpu.make_async_remote_copy(
+            src_ref=source,
+            dst_ref=self.landing[stage].at[:, rows, :],
+            send_sem=self.send.at[stage, part],
+            recv_sem=self.recv.at[stage, part],
+            device_id=target,
+            device_id_type=MESH,
+        )
+
+    def start(self, stage, part):
+        self.copy(stage, part).start()
+
+    def finish(self, stage, part):
+        place, rows = self.place, self.cut(part)
+        self.copy(stage, part).wait_recv()
+        count = self.blocks.shape[0] >> stage
+        final = stage == len(self.bits)
+
+        def add(index, carry):
+            if stage == 0:
+                own = self.blocks[index, place.core, rows, :]
+            else:
+                own = self.kept[stage - 1][
+                    place.bit(self.bits[stage - 1]) * count + index, rows, :
+                ]
+            total = own.astype(jnp.float32) + self.landing[stage][index, rows, :].astype(
+                jnp.float32
+            )
+            if final:
+                self.last(index, rows, total)
+            else:
+                self.kept[stage][index, rows, :] = total.astype(jnp.bfloat16)
+            return carry
+
+        lax.fori_loop(0, count, add, 0)
+
+    def drain(self):
+        for stage in range(len(self.bits) + 1):
+            for part in range(self.parts):
+                self.copy(stage, part).wait_send()
+
+
+class Place:
+    def __init__(self, ranks):
+        self.ranks = ranks
+        self.rank = lax.axis_index("wide")
+        self.core = lax.axis_index("rep")
+        self.other_core = (self.rank, 1 - self.core)
+
+    def bit(self, index):
+        return (self.rank // (1 << index)) % 2
+
+    def across(self, index):
+        step = 1 << index
+        return (self.rank + step - 2 * step * self.bit(index), self.core)
+
+
+def block_order(ranks, order):
+    places = []
+    for rank in range(ranks):
+        spot = 0
+        for bit in order:
+            spot = spot * 2 + (rank >> bit) % 2
+        places.append(spot)
+    return places
+
+
+def fused_kernel(names, ranks, table_rows, *refs):
+    s = types.SimpleNamespace(**dict(zip(names, refs, strict=True)))
+    place = Place(ranks)
+    bits = (ranks - 1).bit_length()
+    far = list(range(2, bits))
+    images_here, pixels, channels = s.arrived.shape
+    flat_rows = images_here * pixels
+    piece = pixels // ranks
+    half = channels // 2
+    steps = pixels // CHUNK
+    score_scale = channels ** (-0.5)
+    count_inverse = 1.0 / (pixels * (channels // GROUPS))
+    col = lax.broadcasted_iota(jnp.int32, (CHUNK, 1), 0) % SIDE
+
+    loads = []
+    for index, name in enumerate(
+        ("noise_table", "embed_weight", "conv_one", "conv_two", "query_weight", "key_weight", "value_weight", "out_weight")
+    ):
+        source = getattr(s, name)
+        target = getattr(s, name + "_here")
+        if name == "noise_table":
+            target = target.at[pl.ds(0, table_rows), :]
+        loads.append(pltpu.make_async_copy(source, target, s.load_sem.at[index]))
+        loads[-1].start()
+
+    barrier = pltpu.get_barrier_semaphore()
+
+    def greet(offset, carry):
+        pl.semaphore_signal(
+            barrier,
+            inc=1,
+            device_id=((place.rank + offset) % ranks, place.core),
+            device_id_type=MESH,
+        )
+        return carry
+
+    lax.fori_loop(1, ranks, greet, 0)
+    pl.semaphore_signal(barrier, inc=1, device_id=place.other_core, device_id_type=MESH)
+    pl.semaphore_wait(barrier, ranks)
+
+    def gather_copy(which, source, target, offset):
+        peer = (place.rank + offset) % ranks
+        return pltpu.make_async_remote_copy(
+            src_ref=source.at[pl.ds(peer * images_here, images_here)],
+            dst_ref=target.at[:, pl.ds(pl.multiple_of(place.rank * piece, 16), piece)],
+            send_sem=s.swap_send.at[which, offset],
+            recv_sem=s.swap_recv.at[which, offset],
+            device_id=(peer, place.core),
+            device_id_type=MESH,
+        )
+
+    def gather_own(which, source, target):
+        return pltpu.make_async_copy(
+            source.at[pl.ds(place.rank * images_here, images_here)],
+            target.at[:, pl.ds(pl.multiple_of(place.rank * piece, 16), piece)],
+            s.swap_own.at[which],
+        )
+
+    def scatter_copy(which, source, target, offset):
+        peer = (place.rank + offset) % ranks
+        return pltpu.make_async_remote_copy(
+            src_ref=source.at[:, pl.ds(pl.multiple_of(peer * piece, 16), piece)],
+            dst_ref=target.at[pl.ds(place.rank * images_here, images_here)],
+            send_sem=s.swap_send.at[which, offset],
+            recv_sem=s.swap_recv.at[which, offset],
+            device_id=(peer, place.core),
+            device_id_type=MESH,
+        )
+
+    def scatter_own(which, source, target):
+        return pltpu.make_async_copy(
+            source.at[:, pl.ds(pl.multiple_of(place.rank * piece, 16), piece)],
+            target.at[pl.ds(place.rank * images_here, images_here)],
+            s.swap_own.at[which],
+        )
+
+    def swap_start(copy, own, which, source, target):
+        def go(offset, carry):
+            copy(which, source, target, offset).start()
+            return carry
+
+        lax.fori_loop(1, ranks, go, 0)
+        own(which, source, target).start()
+
+    def swap_arrive(copy, own, which, source, target):
+        def go(offset, carry):
+            copy(which, source, target, offset).wait_recv()
+            return carry
+
+        lax.fori_loop(1, ranks, go, 0)
+        own(which, source, target).wait()
+
+    def swap_drain(copy, which, source, target):
+        def go(offset, carry):
+            copy(which, source, target, offset).wait_send()
+            return carry
+
+        lax.fori_loop(1, ranks, go, 0)
+
+    swap_start(gather_copy, gather_own, 0, s.images, s.arrived)
+
+    for padded in (s.spread_act, s.spread_two, s.spread_one, s.spread_far):
+        for image in range(images_here):
+            edge = jnp.zeros((SIDE, padded.shape[2]), jnp.bfloat16)
+            padded[image, 0:SIDE, :] = edge
+            padded[image, pixels + SIDE : pixels + 2 * SIDE, :] = edge
+    tail = s.noise_table_here.shape[0] - table_rows
+    if tail:
+        s.noise_table_here[table_rows:, :] = jnp.zeros((tail, channels), jnp.bfloat16)
+    own_levels = [s.levels[place.rank * images_here + image] for image in range(images_here)]
+    entry = lax.broadcasted_iota(jnp.int32, (8, s.noise_table_here.shape[0]), 1)
+    line = lax.broadcasted_iota(jnp.int32, entry.shape, 0)
+    selected = jnp.zeros(entry.shape, jnp.float32)
+    for image in range(images_here):
+        hit = jnp.where(entry == own_levels[image], 1.0, 0.0)
+        selected = jnp.where(line == image, hit, selected)
+    loads[0].wait()
+    loads[1].wait()
+    embedded = matmul(selected.astype(jnp.bfloat16), s.noise_table_here[...])
+    embed_shift = matmul(embedded.astype(jnp.bfloat16), s.embed_weight_here[...])
+    embed_shift = embed_shift + s.embed_bias[...] + s.bias_one[...]
+
+    def over(image, body, start):
+        return lax.fori_loop(0, steps, functools.partial(body, image), start)
+
+    def at(step):
+        return pl.ds(pl.multiple_of(step * CHUNK, CHUNK), CHUNK)
+
+    def flat_at(image, step):
+        return pl.ds(pl.multiple_of(image * pixels + step * CHUNK, CHUNK), CHUNK)
+
+    def fold(chunk):
+        return jnp.sum(chunk.reshape(CHUNK // 8, 8, channels), axis=0)
+
+    none = jnp.zeros((8, channels), jnp.float32)
+
+    def whole(part):
+        return jnp.sum(part, axis=0, keepdims=True)
+
+    def statistics(load):
+        def first(image, step, total):
+            return total + fold(load(image, step))
+
+        sums = [whole(over(image, first, none)) for image in range(images_here)]
+        center = group_sum(stack_rows(sums)) * count_inverse
+
+        def second(image, step, total):
+            spread = load(image, step) - center[image : image + 1]
+            return total + fold(spread * spread)
+
+        sums = [whole(over(image, second, none)) for image in range(images_here)]
+        variance = group_sum(stack_rows(sums)) * count_inverse
+        return center, lax.rsqrt(variance + epsilon)
+
+    def spread_out(target, image, step, chunk, before, after):
+        width = chunk.shape[1]
+        rows = pl.ds(pl.multiple_of(step * CHUNK + SIDE, SIDE), CHUNK)
+        target[image, rows, before * width : (before + 1) * width] = jnp.where(
+            col > 0, pltpu.roll(chunk, 1, 0), 0.0
+        ).astype(jnp.bfloat16)
+        target[image, rows, width : 2 * width] = chunk.astype(jnp.bfloat16)
+        target[image, rows, after * width : (after + 1) * width] = jnp.where(
+            col < SIDE - 1, pltpu.roll(chunk, CHUNK - 1, 0), 0.0
+        ).astype(jnp.bfloat16)
+
+    def activate(load, center, rate, gain, shift, keep):
+        for image in range(images_here):
+            slope = rate[image : image + 1] * gain
+
+            def apply(image, step, carry, slope=slope):
+                field = (load(image, step) - center[image : image + 1]) * slope + shift
+                act = field * sigmoid(field)
+                spread_out(s.spread_act, image, step, act, 0, 2)
+                keep[flat_at(image, step), :] = act.astype(jnp.bfloat16)
+                return carry
+
+            over(image, apply, 0)
+
+    def convolve(weight):
+        total = None
+        for row_tap in range(3):
+            window = s.spread_act[:, SIDE * row_tap : SIDE * row_tap + pixels, :]
+            term = matmul(
+                window.reshape(flat_rows, 3 * channels),
+                weight[3 * channels * row_tap : 3 * channels * (row_tap + 1), :],
+            )
+            total = term if total is None else total + term
+        return total
+
+    def tap_rows(row_tap):
+        return slice(SIDE * (2 - row_tap), SIDE * (2 - row_tap) + pixels)
+
+    def convolve_back(source, weight):
+        total = None
+        for tap in range(9):
+            window = source[
+                :, tap_rows(tap // 3), (tap % 3) * channels : (tap % 3 + 1) * channels
+            ]
+            term = against(
+                window.reshape(flat_rows, channels),
+                weight[channels * tap : channels * (tap + 1), :],
+            )
+            total = term if total is None else total + term
+        return total
+
+    def share_copy(slot, source, target, bit):
+        return pltpu.make_async_remote_copy(
+            src_ref=source,
+            dst_ref=target,
+            send_sem=s.share_send.at[slot],
+            recv_sem=s.share_recv.at[slot],
+            device_id=place.across(bit),
+            device_id_type=MESH,
+        )
+
+    bit_one, bit_two = 1, 0
+    half_one, half_two = place.bit(bit_one), place.bit(bit_two)
+
+    def other_half(ref, mine):
+        return ref.at[:, pl.ds(pl.multiple_of((1 - mine) * half, half), half)]
+
+    share_act_one = share_copy(0, s.act_one, s.act_one_far, bit_one)
+    share_act_two = share_copy(1, s.act_two, s.act_two_far, bit_two)
+    share_grad_two = share_copy(2, other_half(s.grad_two, half_two), s.grad_two_far, bit_two)
+    share_grad_one = share_copy(3, other_half(s.grad_one, half_one), s.grad_one_far, bit_one)
+
+    def weigh(spread, mine, act, act_far, grad_far, blocks, spots):
+        def unfold(image, step, carry):
+            chunk = grad_far[flat_at(image, step), :].astype(jnp.float32)
+            spread_out(s.spread_far, image, step, chunk, 2, 0)
+            return carry
+
+        for image in range(images_here):
+            over(image, unfold, 0)
+        rows_block = blocks.shape[2]
+        for tap in range(9):
+            rows, side_tap = tap_rows(tap // 3), tap % 3
+            near = spread[
+                :, rows, pl.ds(pl.multiple_of(side_tap * channels + mine * half, half), half)
+            ]
+            beyond = s.spread_far[:, rows, side_tap * half : (side_tap + 1) * half]
+            product = by_rows(act[...], near.reshape(flat_rows, half)) + by_rows(
+                act_far[...], beyond.reshape(flat_rows, half)
+            )
+            product = product.astype(jnp.bfloat16)
+            done = 0
+            while done < channels:
+                block, inside = divmod(tap * channels + done, rows_block)
+                size = min(rows_block - inside, channels - done)
+                blocks[spots[block // 2], block % 2, inside : inside + size, :] = product[
+                    done : done + size
+                ]
+                done = done + size
+
+    def last_conv(share, kept):
+        def put(index, rows, total):
+            kept[index, rows, :] = total
+
+        return put
+
+    order_one = [1 - bit_one] + far
+    order_two = [1 - bit_two] + far
+    order_mix = [0, 1] + far
+    spots_one = block_order(ranks, order_one + [bit_one])
+    spots_two = block_order(ranks, order_two + [bit_two])
+    spots_mix = block_order(ranks, order_mix)
+
+    def put_one(index, rows, total):
+        s.sum_one[index, rows, :] = total
+        s.fin_one[index, rows, :] = total.astype(jnp.bfloat16)
+
+    def put_two(index, rows, total):
+        s.sum_two[index, rows, :] = total
+        s.fin_two[index, rows, :] = total.astype(jnp.bfloat16)
+
+    def put_mix(index, rows, total):
+        s.share_mix[rows, :] = total
+
+    def gathered(name, count):
+        return [getattr(s, f"{name}_{index}") for index in range(count)]
+
+    parts = s.reduce_send_one.shape[1]
+    reduce_one = Reduce(
+        place,
+        s.blocks_one,
+        order_one,
+        gathered("land_one", bits),
+        gathered("kept_one", bits - 1),
+        s.reduce_send_one,
+        s.reduce_recv_one,
+        parts,
+        put_one,
+    )
+    reduce_two = Reduce(
+        place,
+        s.blocks_two,
+        order_two,
+        gathered("land_two", bits),
+        gathered("kept_two", bits - 1),
+        s.reduce_send_two,
+        s.reduce_recv_two,
+        parts,
+        put_two,
+    )
+    reduce_mix = Reduce(
+        place,
+        s.blocks_mix,
+        order_mix,
+        gathered("land_mix", bits + 1),
+        gathered("kept_mix", bits),
+        s.reduce_send_mix,
+        s.reduce_recv_mix,
+        1,
+        put_mix,
+    )
+
+    def last_copy(slot, fin, target, mine, bit):
+        return share_copy(slot, fin.at[1 - mine], target, bit)
+
+    def settle(copy, sums, target, mine, share):
+        copy.wait_recv()
+        own = sums[mine]
+        other = target[...].astype(jnp.float32)
+        share[:, 0:half] = jnp.where(mine == 0, own, other)
+        share[:, half:channels] = jnp.where(mine == 0, other, own)
+
+    def small_copy(stage):
+        return pltpu.make_async_remote_copy(
+            src_ref=s.small_sum.at[stage],
+            dst_ref=s.small_land.at[stage],
+            send_sem=s.small_send.at[stage],
+            recv_sem=s.small_recv.at[stage],
+            device_id=place.other_core if stage == 0 else place.across(stage - 1),
+            device_id_type=MESH,
+        )
+
+    def small_finish(stage):
+        small_copy(stage).wait_recv()
+        s.small_sum[stage + 1] = s.small_sum[stage] + s.small_land[stage]
+
+    slot_rows = 16
+    device = place.rank * 2 + place.core
+
+    def slots_copy(stage):
+        count = 1 << stage
+        first = pl.multiple_of((device // count) * count * slot_rows, slot_rows)
+        window = s.slots.at[pl.ds(first, count * slot_rows), :]
+        return pltpu.make_async_remote_copy(
+            src_ref=window,
+            dst_ref=window,
+            send_sem=s.slots_send.at[stage],
+            recv_sem=s.slots_recv.at[stage],
+            device_id=place.other_core if stage == 0 else place.across(stage - 1),
+            device_id_type=MESH,
+        )
+
+    swap_arrive(gather_copy, gather_own, 0, s.images, s.arrived)
+    swap_start(gather_copy, gather_own, 1, s.cotangent, s.upstream)
+
+    def load_input(image, step):
+        return s.arrived[image, at(step), :].astype(jnp.float32)
+
+    def load_hidden(image, step):
+        return s.hidden[flat_at(image, step), :]
+
+    def load_middle(image, step):
+        return s.middle[flat_at(image, step), :]
+
+    gain_one, shift_one = s.gain_one[...], s.shift_one[...]
+    gain_two, shift_two = s.gain_two[...], s.shift_two[...]
+    gain_three, shift_three = s.gain_three[...], s.shift_three[...]
+    center_one, rate_one = statistics(load_input)
+    activate(load_input, center_one, rate_one, gain_one, shift_one, s.act_one)
+    share_act_one.start()
+    loads[2].wait()
+    conv = convolve(s.conv_one_here)
+    for image in range(images_here):
+        rows = slice(image * pixels, (image + 1) * pixels)
+        s.hidden[rows, :] = conv[rows] + embed_shift[image : image + 1]
+    center_two, rate_two = statistics(load_hidden)
+    activate(load_hidden, center_two, rate_two, gain_two, shift_two, s.act_two)
+    share_act_two.start()
+    loads[3].wait()
+    s.middle[...] = (
+        convolve(s.conv_two_here)
+        + s.bias_two[...]
+        + s.arrived[...].reshape(flat_rows, channels).astype(jnp.float32)
+    )
+    center_three, rate_three = statistics(load_middle)
+    for image in range(images_here):
+        slope = rate_three[image : image + 1] * gain_three
+
+        def normalize(image, step, carry, slope=slope):
+            spread = load_middle(image, step) - center_three[image : image + 1]
+            s.normed[flat_at(image, step), :] = (spread * slope + shift_three).astype(jnp.bfloat16)
+            return carry
+
+        over(image, normalize, 0)
+    for load in loads[4:]:
+        load.wait()
+    normed = s.normed[...]
+    s.query[...] = (matmul(normed, s.query_weight_here[...]) + s.query_bias[...]).astype(
+        jnp.bfloat16
+    )
+    s.key[...] = matmul(normed, s.key_weight_here[...]).astype(jnp.bfloat16)
+    s.value[...] = (matmul(normed, s.value_weight_here[...]) + s.value_bias[...]).astype(
+        jnp.bfloat16
+    )
+    for image in range(images_here):
+        rows = slice(image * pixels, (image + 1) * pixels)
+        scores = against(s.query[rows, :], s.key[rows, :]) * score_scale
+        exponent = jnp.exp(scores - jnp.max(scores, axis=1, keepdims=True))
+        probs = exponent / jnp.sum(exponent, axis=1, keepdims=True)
+        s.probs[rows, :] = probs
+        s.mixed[rows, :] = matmul(probs.astype(jnp.bfloat16), s.value[rows, :]).astype(
+            jnp.bfloat16
+        )
+    result = s.middle[...] + matmul(s.mixed[...], s.out_weight_here[...]) + s.out_bias[...]
+    s.leaving[...] = result.astype(jnp.bfloat16).reshape(images_here, pixels, channels)
+
+    swap_arrive(gather_copy, gather_own, 1, s.cotangent, s.upstream)
+    swap_start(scatter_copy, scatter_own, 2, s.leaving, s.output)
+
+    def load_upstream(image, step):
+        return s.upstream[image, at(step), :].astype(jnp.float32)
+
+    def column_sums(load):
+        def body(image, step, total):
+            return total + fold(load(image, step))
+
+        total = none
+        for image in range(images_here):
+            total = over(image, body, total)
+        return whole(total)
+
+    grad_out_bias = column_sums(load_upstream)
+    upstream = s.upstream[...].reshape(flat_rows, channels)
+    mix_rows = s.blocks_mix.shape[2] // 4
+
+    def store_mix(which, product):
+        product = product.astype(jnp.bfloat16)
+        for rank in range(ranks):
+            for core in range(2):
+                block = rank * 2 + core
+                s.blocks_mix[
+                    spots_mix[rank], core, which * mix_rows : (which + 1) * mix_rows, :
+                ] = product[block * mix_rows : (block + 1) * mix_rows]
+
+    store_mix(3, by_rows(s.mixed[...], upstream))
+    s.grad_mixed[...] = against(upstream, s.out_weight_here[...]).astype(jnp.bfloat16)
+    for image in range(images_here):
+        rows = slice(image * pixels, (image + 1) * pixels)
+        probs = s.probs[rows, :]
+        grad_mixed = s.grad_mixed[rows, :]
+        grad_probs = against(grad_mixed, s.value[rows, :])
+        s.grad_value[rows, :] = by_rows(probs.astype(jnp.bfloat16), grad_mixed).astype(
+            jnp.bfloat16
+        )
+        inner = jnp.sum(grad_probs * probs, axis=1, keepdims=True)
+        grad_scores = (probs * (grad_probs - inner)).astype(jnp.bfloat16)
+        s.grad_query[rows, :] = (matmul(grad_scores, s.key[rows, :]) * score_scale).astype(
+            jnp.bfloat16
+        )
+        s.grad_key[rows, :] = (by_rows(grad_scores, s.query[rows, :]) * score_scale).astype(
+            jnp.bfloat16
+        )
+
+    s.delta[...] = (
+        against(s.grad_query[...], s.query_weight_here[...])
+        + against(s.grad_key[...], s.key_weight_here[...])
+        + against(s.grad_value[...], s.value_weight_here[...])
+    )
+
+    def delta_at(image, step):
+        return s.delta[flat_at(image, step), :]
+
+    def norm_back_terms(gain, shift_sums, gain_sums):
+        rows = [gain * total for total in shift_sums] + [gain * total for total in gain_sums]
+        return group_sum(stack_rows(rows)) * count_inverse
+
+    shift_sums, gain_sums = [], []
+    for image in range(images_here):
+
+        def sums_three(image, step, totals):
+            grad = delta_at(image, step)
+            unit = (load_middle(image, step) - center_three[image : image + 1]) * rate_three[
+                image : image + 1
+            ]
+            return totals[0] + fold(grad), totals[1] + fold(grad * unit)
+
+        totals = over(image, sums_three, (none, none))
+        shift_sums.append(whole(totals[0]))
+        gain_sums.append(whole(totals[1]))
+    means = norm_back_terms(gain_three, shift_sums, gain_sums)
+    grad_gain_three = functools.reduce(jnp.add, gain_sums)
+    grad_shift_three = functools.reduce(jnp.add, shift_sums)
+    total_two = none
+    for image in range(images_here):
+        mean_shift = means[image : image + 1]
+        mean_gain = means[images_here + image : images_here + image + 1]
+
+        def back_three(image, step, total, mean_shift=mean_shift, mean_gain=mean_gain):
+            rate = rate_three[image : image + 1]
+            unit = (load_middle(image, step) - center_three[image : image + 1]) * rate
+            grad = rate * (delta_at(image, step) * gain_three - mean_shift - unit * mean_gain)
+            grad = grad + load_upstream(image, step)
+            s.grad_middle[flat_at(image, step), :] = grad
+            low = grad.astype(jnp.bfloat16)
+            s.grad_two[flat_at(image, step), :] = low
+            low = low.astype(jnp.float32)
+            spread_out(s.spread_two, image, step, low, 2, 0)
+            return total + fold(low)
+
+        total_two = over(image, back_three, total_two)
+    grad_bias_two = whole(total_two)
+    share_grad_two.start()
+
+    store_mix(0, by_rows(normed, s.grad_query[...]))
+    store_mix(1, by_rows(normed, s.grad_key[...]))
+    store_mix(2, by_rows(normed, s.grad_value[...]))
+    reduce_mix.start(0, 0)
+
+    def load_grad(ref):
+        return lambda image, step: ref[flat_at(image, step), :].astype(jnp.float32)
+
+    grad_query_bias = column_sums(load_grad(s.grad_query))
+    grad_value_bias = column_sums(load_grad(s.grad_value))
+
+    def swish_norm_back(load, center, rate, gain, shift, put, start):
+        shift_sums, gain_sums = [], []
+        for image in range(images_here):
+
+            def sums(image, step, totals):
+                unit = (load(image, step) - center[image : image + 1]) * rate[image : image + 1]
+                field = unit * gain + shift
+                gate = sigmoid(field)
+                grad = delta_at(image, step) * (gate * (1.0 + field * (1.0 - gate)))
+                s.delta[flat_at(image, step), :] = grad
+                return totals[0] + fold(grad), totals[1] + fold(grad * unit)
+
+            totals = over(image, sums, (none, none))
+            shift_sums.append(whole(totals[0]))
+            gain_sums.append(whole(totals[1]))
+        means = norm_back_terms(gain, shift_sums, gain_sums)
+        carries = []
+        for image in range(images_here):
+            mean_shift = means[image : image + 1]
+            mean_gain = means[images_here + image : images_here + image + 1]
+
+            def back(image, step, carry, mean_shift=mean_shift, mean_gain=mean_gain):
+                slope = rate[image : image + 1]
+                unit = (load(image, step) - center[image : image + 1]) * slope
+                grad = slope * (delta_at(image, step) * gain - mean_shift - unit * mean_gain)
+                return put(image, step, grad, carry)
+
+            carries.append(over(image, back, start))
+        return (
+            functools.reduce(jnp.add, gain_sums),
+            functools.reduce(jnp.add, shift_sums),
+            carries,
+        )
+
+    s.delta[...] = convolve_back(s.spread_two, s.conv_two_here)
+
+    def put_hidden(image, step, grad, total):
+        low = grad.astype(jnp.bfloat16)
+        s.grad_one[flat_at(image, step), :] = low
+        low = low.astype(jnp.float32)
+        spread_out(s.spread_one, image, step, low, 2, 0)
+        return total + fold(low)
+
+    grad_gain_two, grad_shift_two, totals = swish_norm_back(
+        load_hidden, center_two, rate_two, gain_two, shift_two, put_hidden, none
+    )
+    share_grad_one.start()
+    grad_shift = [whole(total) for total in totals]
+    grad_bias_one = functools.reduce(jnp.add, grad_shift)
+
+    lanes = s.slots.shape[1]
+    slot_place = lax.broadcasted_iota(jnp.int32, (slot_rows, lanes), 0)
+    slot = jnp.zeros((slot_rows, lanes), jnp.float32)
+    per_image = channels // lanes
+    for image in range(images_here):
+        for index in range(per_image):
+            row = grad_shift[image][:, index * lanes : (index + 1) * lanes]
+            slot = jnp.where(
+                slot_place == image * per_image + index, jnp.broadcast_to(row, slot.shape), slot
+            )
+        slot = jnp.where(
+            slot_place == images_here * per_image + image,
+            own_levels[image].astype(jnp.float32),
+            slot,
+        )
+    s.slots[pl.ds(pl.multiple_of(device * slot_rows, slot_rows), slot_rows), :] = slot
+    slots_copy(0).start()
+
+    reduce_mix.finish(0, 0)
+    reduce_mix.start(1, 0)
+    slots_copy(0).wait_recv()
+    slots_copy(1).start()
+
+    share_act_two.wait_recv()
+    share_grad_two.wait_recv()
+    weigh(
+        s.spread_two, half_two, s.act_two, s.act_two_far, s.grad_two_far, s.blocks_two, spots_two
+    )
+    for part in range(parts):
+        reduce_two.start(0, part)
+
+    s.delta[...] = convolve_back(s.spread_one, s.conv_one_here)
+
+    def put_input(image, step, grad, carry):
+        total = grad + s.grad_middle[flat_at(image, step), :]
+        s.leaving_grad[image, at(step), :] = total.astype(jnp.bfloat16)
+        return carry
+
+    grad_gain_one, grad_shift_one, _ = swish_norm_back(
+        load_input, center_one, rate_one, gain_one, shift_one, put_input, 0
+    )
+    swap_start(scatter_copy, scatter_own, 3, s.leaving_grad, s.input_grad)
+
+    sums = dict(
+        gain_one=grad_gain_one,
+        shift_one=grad_shift_one,
+        bias_one=grad_bias_one,
+        gain_two=grad_gain_two,
+        shift_two=grad_shift_two,
+        bias_two=grad_bias_two,
+        gain_three=grad_gain_three,
+        shift_three=grad_shift_three,
+        query_bias=grad_query_bias,
+        value_bias=grad_value_bias,
+        out_bias=grad_out_bias,
+    )
+    rows = [sums[name] for name in SUMS]
+    s.small_sum[0, 0:8, :] = stack_rows(rows[:8])
+    s.small_sum[0, 8:16, :] = stack_rows(rows[8:])
+    small_copy(0).start()
+
+    for part in range(parts):
+        reduce_two.finish(0, part)
+        reduce_two.start(1, part)
+    share_act_one.wait_recv()
+    share_grad_one.wait_recv()
+    weigh(
+        s.spread_one, half_one, s.act_one, s.act_one_far, s.grad_one_far, s.blocks_one, spots_one
+    )
+    for part in range(parts):
+        reduce_one.start(0, part)
+
+    reduce_mix.finish(1, 0)
+    reduce_mix.start(2, 0)
+    slots_copy(1).wait_recv()
+    slots_copy(2).start()
+    small_finish(0)
+    small_copy(1).start()
+    for part in range(parts):
+        reduce_one.finish(0, part)
+        reduce_one.start(1, part)
+    for stage in range(1, bits):
+        for part in range(parts):
+            reduce_two.finish(stage, part)
+            if stage + 1 < bits:
+                reduce_two.start(stage + 1, part)
+        if stage + 1 <= bits:
+            reduce_mix.finish(stage + 1, 0)
+            if stage + 2 <= bits:
+                reduce_mix.start(stage + 2, 0)
+        slots_copy(stage + 1).wait_recv()
+        if stage + 2 <= bits:
+            slots_copy(stage + 2).start()
+        small_finish(stage)
+        small_copy(stage + 1).start()
+        for part in range(parts):
+            reduce_one.finish(stage, part)
+            if stage + 1 < bits:
+                reduce_one.start(stage + 1, part)
+    small_finish(bits)
+    end_two = last_copy(4, s.fin_two, s.last_two, half_two, bit_two)
+    end_one = last_copy(5, s.fin_one, s.last_one, half_one, bit_one)
+    end_two.start()
+    end_one.start()
+    s.sums[...] = s.small_sum[bits + 1]
+    s.slots_out[...] = s.slots[...]
+    settle(end_two, s.sum_two, s.last_two, half_two, s.share_two)
+    settle(end_one, s.sum_one, s.last_one, half_one, s.share_one)
+    swap_arrive(scatter_copy, scatter_own, 2, s.leaving, s.output)
+    swap_arrive(scatter_copy, scatter_own, 3, s.leaving_grad, s.input_grad)
+
+    swap_drain(gather_copy, 0, s.images, s.arrived)
+    swap_drain(gather_copy, 1, s.cotangent, s.upstream)
+    swap_drain(scatter_copy, 2, s.leaving, s.output)
+    swap_drain(scatter_copy, 3, s.leaving_grad, s.input_grad)
+    for copy in (share_act_one, share_act_two, share_grad_two, share_grad_one, end_two, end_one):
+        copy.wait_send()
+    for reduction in (reduce_mix, reduce_two, reduce_one):
+        reduction.drain()
+    for stage in range(bits + 1):
+        small_copy(stage).wait_send()
+        slots_copy(stage).wait_send()
+
+
+def last_kernel(names, table_rows, *refs):
+    s = types.SimpleNamespace(**dict(zip(names, refs, strict=True)))
+    device = lax.axis_index("wide") * lax.axis_size("rep") + lax.axis_index("rep")
+    moves = [
+        pltpu.make_async_copy(s.output_in, s.output, s.sems.at[0]),
+        pltpu.make_async_copy(s.input_grad_in, s.input_grad, s.sems.at[1]),
+    ]
+    for move in moves:
+        move.start()
+    lanes = s.slots.shape[1]
+    channels = s.embed_weight.shape[0]
+    per_image = channels // lanes
+
+    def flat(target, rows, first=0):
+        count = rows.shape[0]
+        width = rows.shape[1] // lanes
+        for index in range(width):
+            target[pl.ds(first + index, count, stride=width), :] = rows[
+                :, index * lanes : (index + 1) * lanes
+            ]
+
+    flat(s.conv_one, s.share_one[...])
+    flat(s.conv_two, s.share_two[...])
+    mix_rows = s.share_mix.shape[0] // 4
+    for index, target in enumerate((s.query, s.key, s.value, s.out)):
+        flat(target, s.share_mix[index * mix_rows : (index + 1) * mix_rows, :])
+    for index, name in enumerate(SUMS):
+        getattr(s, "sum_" + name)[...] = s.sums[index : index + 1, :]
+    s.sum_embed_bias[...] = s.sums[SUMS.index("bias_one") : SUMS.index("bias_one") + 1, :]
+
+    slot_rows = 16
+    devices = s.slots.shape[0] // slot_rows
+    images_here = 2
+
+    def every(index):
+        return s.slots[pl.ds(index, devices, stride=slot_rows), :]
+
+    de = jnp.concatenate(
+        [
+            jnp.concatenate([every(image * per_image + j) for j in range(per_image)], axis=1)
+            for image in range(images_here)
+        ],
+        axis=0,
+    )
+    levels = jnp.concatenate(
+        [every(images_here * per_image + image) for image in range(images_here)], axis=0
+    ).astype(jnp.int32)
+    padded_rows = s.noise_table.shape[0]
+    entry = lax.broadcasted_iota(jnp.int32, (levels.shape[0], padded_rows), 1)
+    hit = jnp.where(entry == levels[:, 0:1], 1.0, 0.0).astype(jnp.bfloat16)
+    embedded = matmul(hit, s.noise_table[...])
+    exact = dict(preferred_element_type=jnp.float32, precision=lax.Precision.HIGHEST)
+    own_rows = s.embed.shape[0] * lanes // channels
+    s.product[...] = lax.dot_general(embedded, de, (((0,), (0,)), ((), ())), **exact)
+    flat(s.embed, s.product[pl.ds(pl.multiple_of(device * own_rows, own_rows), own_rows), :])
+    grad_rows = lax.dot_general(
+        de, s.embed_weight[...].astype(jnp.float32), (((1,), (1,)), ((), ())), **exact
+    )
+    half = channels // 2
+    halves = s.table.shape[0] * lanes // half
+    wide = -(-halves // 128) * 128
+    spot = lax.broadcasted_iota(jnp.int32, (levels.shape[0], wide), 1) + device * halves
+    total = jnp.zeros((wide, half), jnp.float32)
+    for side in range(2):
+        pick = jnp.where(2 * levels[:, 0:1] + side == spot, 1.0, 0.0)
+        total = total + lax.dot_general(
+            pick, grad_rows[:, side * half : (side + 1) * half], (((0,), (0,)), ((), ())), **exact
+        )
+    flat(s.table, total[:halves])
+    for move in moves:
+        move.wait()
+
+
+def fused_device(*operands):
+    given = dict(zip(ARGUMENTS, operands, strict=True))
+    ranks = lax.axis_size("wide")
+    bits = (ranks - 1).bit_length()
+    images = given["images"]
+    images_rep, piece, channels = images.shape
+    images_here, pixels = images_rep // ranks, piece * ranks
+    flat_rows = images_here * pixels
+    half = channels // 2
+    devices = ranks * 2
+    table_rows = given["noise_table"].shape[0]
+    padded_rows = -(-table_rows // 128) * 128
+    conv_rows = given["conv_one"].shape[0] // devices
+    mix_rows = 4 * channels // devices
+    low, full = jnp.bfloat16, jnp.float32
+    parts = 3 if conv_rows % 48 == 0 else 1
+
+    def struct(shape, kind):
+        return jax.ShapeDtypeStruct(shape, kind)
+
+    outputs = dict(
+        output=struct(images.shape, low),
+        input_grad=struct(images.shape, low),
+        share_one=struct((conv_rows, channels), full),
+        share_two=struct((conv_rows, channels), full),
+        share_mix=struct((mix_rows, channels), full),
+        sums=struct((16, channels), full),
+        slots_out=struct((devices * 16, 128), full),
+    )
+    flat_low, flat_full = (flat_rows, channels), (flat_rows, channels)
+    padded = pixels + 2 * SIDE
+    scratch = dict(
+        noise_table_here=pltpu.VMEM((padded_rows, channels), low),
+        embed_weight_here=pltpu.VMEM((channels, channels), low),
+        conv_one_here=pltpu.VMEM(given["conv_one"].shape, low),
+        conv_two_here=pltpu.VMEM(given["conv_two"].shape, low),
+        query_weight_here=pltpu.VMEM((channels, channels), low),
+        key_weight_here=pltpu.VMEM((channels, channels), low),
+        value_weight_here=pltpu.VMEM((channels, channels), low),
+        out_weight_here=pltpu.VMEM((channels, channels), low),
+        arrived=pltpu.VMEM((images_here, pixels, channels), low),
+        upstream=pltpu.VMEM((images_here, pixels, channels), low),
+        leaving=pltpu.VMEM((images_here, pixels, channels), low),
+        leaving_grad=pltpu.VMEM((images_here, pixels, channels), low),
+        spread_act=pltpu.VMEM((images_here, padded, 3 * channels), low),
+        spread_two=pltpu.VMEM((images_here, padded, 3 * channels), low),
+        spread_one=pltpu.VMEM((images_here, padded, 3 * channels), low),
+        spread_far=pltpu.VMEM((images_here, padded, 3 * half), low),
+        hidden=pltpu.VMEM(flat_full, full),
+        middle=pltpu.VMEM(flat_full, full),
+        delta=pltpu.VMEM(flat_full, full),
+        grad_middle=pltpu.VMEM(flat_full, full),
+        probs=pltpu.VMEM((flat_rows, pixels), full),
+        grad_one_far=pltpu.VMEM((flat_rows, half), low),
+        grad_two_far=pltpu.VMEM((flat_rows, half), low),
+        small_sum=pltpu.VMEM((bits + 2, 16, channels), full),
+        small_land=pltpu.VMEM((bits + 1, 16, channels), full),
+        slots=pltpu.VMEM((devices * 16, 128), full),
+        load_sem=pltpu.SemaphoreType.DMA((8,)),
+        swap_send=pltpu.SemaphoreType.DMA((4, ranks)),
+        swap_recv=pltpu.SemaphoreType.DMA((4, ranks)),
+        swap_own=pltpu.SemaphoreType.DMA((4,)),
+        share_send=pltpu.SemaphoreType.DMA((6,)),
+        share_recv=pltpu.SemaphoreType.DMA((6,)),
+        small_send=pltpu.SemaphoreType.DMA((bits + 1,)),
+        small_recv=pltpu.SemaphoreType.DMA((bits + 1,)),
+        slots_send=pltpu.SemaphoreType.DMA((bits + 1,)),
+        slots_recv=pltpu.SemaphoreType.DMA((bits + 1,)),
+    )
+    for name in ("act_one", "act_two", "act_one_far", "act_two_far", "normed", "query", "key", "value", "mixed", "grad_mixed", "grad_query", "grad_key", "grad_value", "grad_one", "grad_two"):
+        scratch[name] = pltpu.VMEM(flat_low, low)
+    for name in ("one", "two"):
+        scratch["blocks_" + name] = pltpu.VMEM((ranks, 2, conv_rows, half), low)
+        for stage in range(bits):
+            scratch[f"land_{name}_{stage}"] = pltpu.VMEM((ranks >> stage, conv_rows, half), low)
+        for stage in range(bits - 1):
+            scratch[f"kept_{name}_{stage}"] = pltpu.VMEM((ranks >> stage, conv_rows, half), low)
+        scratch["sum_" + name] = pltpu.VMEM((2, conv_rows, half), full)
+        scratch["fin_" + name] = pltpu.VMEM((2, conv_rows, half), low)
+        scratch["last_" + name] = pltpu.VMEM((conv_rows, half), low)
+        scratch["reduce_send_" + name] = pltpu.SemaphoreType.DMA((bits, parts))
+        scratch["reduce_recv_" + name] = pltpu.SemaphoreType.DMA((bits, parts))
+    scratch["blocks_mix"] = pltpu.VMEM((ranks, 2, mix_rows, channels), low)
+    for stage in range(bits + 1):
+        scratch[f"land_mix_{stage}"] = pltpu.VMEM((ranks >> stage, mix_rows, channels), low)
+    for stage in range(bits):
+        scratch[f"kept_mix_{stage}"] = pltpu.VMEM((ranks >> stage, mix_rows, channels), low)
+    scratch["reduce_send_mix"] = pltpu.SemaphoreType.DMA((bits + 1, 1))
+    scratch["reduce_recv_mix"] = pltpu.SemaphoreType.DMA((bits + 1, 1))
+
+    in_hbm = INPUTS[:10]
+    in_specs = [pl.BlockSpec(memory_space=pl.ANY)] * len(in_hbm)
+    in_specs.append(pl.BlockSpec(memory_space=pltpu.SMEM))
+    in_specs.extend([pl.BlockSpec(memory_space=pltpu.VMEM)] * (len(INPUTS) - len(in_hbm) - 1))
+    in_vmem = pl.BlockSpec(memory_space=pltpu.VMEM)
+    anywhere = pl.BlockSpec(memory_space=pl.ANY)
+    names = tuple(INPUTS) + tuple(outputs) + tuple(scratch)
+    arrays = [given[name] for name in INPUTS[:11]] + [
+        given[name].reshape(1, channels) for name in INPUTS[11:]
+    ]
+    made = pl.pallas_call(
+        functools.partial(fused_kernel, names, ranks, table_rows),
+        out_shape=tuple(outputs.values()),
+        in_specs=in_specs,
+        out_specs=(anywhere, anywhere) + (in_vmem,) * (len(outputs) - 2),
+        scratch_shapes=list(scratch.values()),
+        compiler_params=pltpu.CompilerParams(
+            collective_id=0, has_side_effects=True, vmem_limit_bytes=63 << 20
+        ),
+        name="block",
+    )(*arrays)
+    made = dict(zip(outputs, made, strict=True))
+
+    share = given["embed_weight"].size // devices // 128
+    finals = dict(
+        output=struct(images.shape, low),
+        input_grad=struct(images.shape, low),
+        table=struct((given["noise_table"].size // devices // 128, 128), full),
+        conv_one=struct((conv_rows * channels // 128, 128), full),
+        conv_two=struct((conv_rows * channels // 128, 128), full),
+        embed=struct((share, 128), full),
+        query=struct((share, 128), full),
+        key=struct((share, 128), full),
+        value=struct((share, 128), full),
+        out=struct((share, 128), full),
+    )
+    for name in ("gain_one", "shift_one", "bias_one", "embed_bias", "gain_two", "shift_two", "bias_two", "gain_three", "shift_three", "query_bias", "value_bias", "out_bias"):
+        finals["sum_" + name] = struct((1, channels), full)
+    sources = dict(
+        output_in=made["output"],
+        input_grad_in=made["input_grad"],
+        share_one=made["share_one"],
+        share_two=made["share_two"],
+        share_mix=made["share_mix"],
+        sums=made["sums"],
+        slots=made["slots_out"],
+        noise_table=given["noise_table"],
+        embed_weight=given["embed_weight"],
+    )
+    names = tuple(sources) + tuple(finals) + ("product", "sems")
+    results = pl.pallas_call(
+        functools.partial(last_kernel, names, table_rows),
+        out_shape=tuple(finals.values()),
+        in_specs=[anywhere, anywhere] + [in_vmem] * (len(sources) - 2),
+        out_specs=(anywhere, anywhere) + (in_vmem,) * (len(finals) - 2),
+        scratch_shapes=[
+            pltpu.VMEM((channels, channels), full),
+            pltpu.SemaphoreType.DMA((2,)),
+        ],
+        compiler_params=pltpu.CompilerParams(vmem_limit_bytes=32 << 20),
+        name="finish",
+    )(*sources.values())
+    return tuple(results[:2]) + tuple(member.reshape(-1) for member in results[2:])
+
+
+ARGUMENTS = ("images", "cotangent", "levels", "noise_table", "gain_one", "shift_one", "conv_one", "bias_one", "embed_weight", "embed_bias", "gain_two", "shift_two", "conv_two", "bias_two", "gain_three", "shift_three", "query_weight", "query_bias", "key_weight", "value_weight", "value_bias", "out_weight", "out_bias")
+
+
+def per_device(*operands):
+    given = dict(zip(ARGUMENTS, operands, strict=True))
+    ranks, cores = lax.axis_size("wide"), lax.axis_size("rep")
+    images_rep, piece, channels = given["images"].shape
+    devices = ranks * cores
+    conv_rows = given["conv_one"].shape[0]
+    fits = (
+        cores == 2
+        and ranks >= 8
+        and ranks & (ranks - 1) == 0
+        and images_rep == 2 * ranks
+        and piece % 16 == 0
+        and conv_rows % (devices * 16) == 0
+        and channels % (devices * 16) == 0
+        and given["noise_table"].size % (devices * channels // 2) == 0
+    )
+    return fused_device(*operands) if fits else plain_device(*operands)
+
+
 def solution(mesh):
     in_specs = (
         P("rep", "wide", None),

time: 741 us -> 132 us (0.18); the launches traced: 732 us -> 131 us
  waiting for transfers between devices: 402 us -> 0 us
  Pallas kernels: 0 us -> 122 us
  local copies, waits for them, and re-layouts: 126 us -> 8.19 us
  other arithmetic: 66.2 us -> 0 us
  matrix products: 55.6 us -> 0 us
  blocking collectives: 42.8 us -> 0 us
  starting transfers between devices: 23.1 us -> 0 us
  between operations: 15.5 us -> 0.87 us
    unnamed x2 -> x0, waiting for transfers between devices: 371 us -> none
    pallas_call x0 -> x2, Pallas kernels: none -> 122 us  [the longest x1 118 us: fused_device(): pl.pallas_call(functools.partial(fused_kernel, names, ranks, table_rows),...]
    reshape x13 -> x0, local copies, waits for them, and re-layouts: 59.1 us -> none  [the longest x8 30.2 us: per_device(): member.reshape(device_count, -1)]
    dot_general x29 -> x0, matrix products: 55.6 us -> none  [the longest x6 21.3 us: contract_rows(): lax.dot_general(left, right, (((0,), (0,)), ((), ())), preferred_element_...]
    reduce_sum x22 -> x0, other arithmetic: 52.3 us -> none  [the longest x4 13.5 us: group_norm(): center = jnp.mean(grouped, axis=(1, 3), keepdims=True)]
    psum x1 -> x0, blocking collectives: 42.8 us -> none  [per_device(): lax.psum((grad_gain_one, grad_shift_one, grad_bias_one, grad_embed_bias,...]
    all_to_all x4 -> x0, waiting for transfers between devices: 31.2 us -> none  [the longest x1 20.8 us: per_device(): lax.all_to_all(result.reshape(images_here, pixels, channels).astype(jnp.b...]
    unnamed x140 -> x18, local copies, waits for them, and re-layouts: 32.2 us -> 8.19 us
  transfers between devices with their start and end apart: 5 -> 0, of which waited for: 3 -> 0; matrix products, arithmetic and copies ran while one was open for 9% -> 0% of each run, Pallas kernels for 0% -> 0%
where the time goes in v1:
time: 132 us; the launch traced here: 131 us
  Pallas kernels  122 us (92%)
  local copies, waits for them, and re-layouts  8.19 us (6%)
    pallas_call x1, Pallas kernels, fused_device(): pl.pallas_call(functools.partial(fused_kernel, names, ranks, table_rows),...  118 us
    unnamed x18, local copies, waits for them, and re-layouts  8.19 us
    pallas_call x1, Pallas kernels, fused_device(): pl.pallas_call(functools.partial(last_kernel, names, table_rows), out_sha...  4.06 us

profile of v1, /device:TPU:0, one launch (start us, length us, event | category | flops | bytes accessed | tf_op | source)
XLA Modules:
  0.0 131.4 jit_solution(7478538718906212497)
XLA Ops:
  0.7 0.0 copy-start.1
  0.7 118.3 %block.1 = (bf16[32,16,512]{2,1,0:T(8,128)(2,1)}, bf16[32,16,512]{2,1,0:T(8,128)(2,1)}, f32[144,512]{1,0:T(8,128)}, f32[144,512]{1,0:T(8,128)}, f32[64,512]{1,0:...) custom-call(bf16[32,16,512]{2,1,0:T(8,128)(2,1)} %refs_0_.1, bf16[32,16,512]{2,1,0:T(8,128)(2,1)} %refs_1_.1, ...), custom_call_target="tpu_custom_call" | custom-call | tf_op jit(solution)/shard_map/block/pallas_call | solution.py:1273
  118.9 0.0 copy-done.1
  119.0 0.0 copy-start
  119.0 1.6 %copy-done = bf16[2000,512]{1,0:T(8,128)(2,1)S(1)} copy-done((bf16[2000,512]{1,0:T(8,128)(2,1)S(1)}, bf16[2000,512]{1,0:T(8,128)(2,1)}, u32[]{:S(2)}) %copy-start) | copy-done | bytes 2048024
  120.5 0.0 copy-start.2
  120.5 1.0 copy-done.2
  121.6 0.0 copy-start.3
  121.6 1.0 copy-done.3
  122.6 0.0 copy-start.4
  122.6 1.0 copy-done.4
  123.6 0.0 copy-start.5
  123.6 1.0 copy-done.5
  124.5 0.0 copy-start.6
  124.5 0.9 copy-done.6
  125.5 0.0 copy-start.7
  125.5 0.9 copy-done.7
  126.4 0.0 copy-start.8
  126.4 0.8 copy-done.8
  127.2 4.1 %finish.1 = (bf16[32,16,512]{2,1,0:T(8,128)(2,1)}, bf16[32,16,512]{2,1,0:T(8,128)(2,1)}, f32[250,128]{1,0:T(8,128)}, f32[576,128]{1,0:T(8,128)}, f32[576,128]{1,...) custom-call(bf16[32,16,512]{2,1,0:T(8,128)(2,1)S(1)} %copy-done.2, ...), custom_call_target="tpu_custom_call" | custom-call | tf_op jit(solution)/shard_map/finish/pallas_call | solution.py:1313
Async XLA Ops:
  0.7 118.3 %copy-start.1 = (bf16[512,512]{1,0:T(8,128)(2,1)S(1)}, bf16[512,512]{1,0:T(8,128)(2,1)}, u32[]{:S(2)}) copy-start(bf16[512,512]{1,0:T(8,128)(2,1)} %refs_8_.3) | copy-start | bytes 1572868
  119.0 1.6 %copy-start = (bf16[2000,512]{1,0:T(8,128)(2,1)S(1)}, bf16[2000,512]{1,0:T(8,128)(2,1)}, u32[]{:S(2)}) copy-start(bf16[2000,512]{1,0:T(8,128)(2,1)} %refs_7_.3) | copy-start | bytes 6144004
  120.5 1.0 copy-start.2
  121.6 1.0 copy-start.3
  122.6 1.0 copy-start.4
  123.6 1.0 copy-start.5
  124.5 0.9 copy-start.6
  125.5 0.9 copy-start.7
  126.4 0.8 copy-start.8

commit v2 on v0

--- a/solution.py
+++ b/solution.py
@@ -1,10 +1,17 @@
+import functools
+import types
+
 import jax
 import jax.numpy as jnp
 from jax import lax
+from jax.experimental import pallas as pl
+from jax.experimental.pallas import tpu as pltpu
 from jax.sharding import PartitionSpec as P
 
 GROUPS = 32
 SIDE = 16
+MESH = pl.DeviceIdType.MESH
+CHUNK = 64
 
 
 epsilon = 1e-05
@@ -72,7 +79,7 @@
     return summed[:, 1 : SIDE + 1, 1 : SIDE + 1, :].reshape(images_here, SIDE * SIDE, channels)
 
 
-def per_device(
+def plain_device(
     images,
     cotangent,
     levels,
@@ -262,6 +269,1260 @@
     return (output_back, input_back) + large_grads + tuple(small_grads)
 
 
+def by_rows(left, right):
+    return lax.dot_general(
+        left, right, (((0,), (0,)), ((), ())), preferred_element_type=jnp.float32
+    )
+
+
+def group_sum(rows, same_group):
+    width = same_group.shape[0]
+    first = rows.astype(jnp.bfloat16).astype(jnp.float32)
+    rest = rows - first
+    second = rest.astype(jnp.bfloat16).astype(jnp.float32)
+    terms = (first, second, rest - second)
+    spans = [slice(start, start + width) for start in range(0, rows.shape[1], width)]
+    stacked = jnp.concatenate([term[:, span] for span in spans for term in terms], axis=0)
+    summed = matmul(stacked.astype(jnp.bfloat16), same_group)
+    parts = [summed[24 * k : 24 * k + 24] for k in range(len(spans))]
+    return jnp.concatenate([part[0:8] + part[8:16] + part[16:24] for part in parts], axis=1)
+
+
+def stack_rows(members):
+    shape = (8, members[0].shape[1])
+    place = lax.broadcasted_iota(jnp.int32, shape, 0)
+    stacked = jnp.zeros(shape, jnp.float32)
+    for index, member in enumerate(members):
+        stacked = jnp.where(place == index, jnp.broadcast_to(member, shape), stacked)
+    return stacked
+
+
+def sigmoid(field):
+    return 0.5 + 0.5 * jnp.tanh(0.5 * field)
+
+
+SUMS = tuple(
+    dict(
+        gain_one=0,
+        shift_one=0,
+        bias_one=0,
+        gain_two=0,
+        shift_two=0,
+        bias_two=0,
+        gain_three=0,
+        shift_three=0,
+        query_bias=0,
+        value_bias=0,
+        out_bias=0,
+    )
+)
+GIVEN_BACK = SUMS[:3] + SUMS[2:]
+
+
+class Flight:
+    def __init__(self, flights, make, offsets=None, whole=None, own=None):
+        self.flights, self.make, self.offsets, self.own = flights, make, offsets, own
+        self.whole = make if whole is None else whole
+        self.arrived = self.left = False
+
+    def start(self):
+        if self.offsets is None:
+            self.make().start()
+        else:
+
+            def go(offset, carry):
+                self.make(offset).start()
+                return carry
+
+            lax.fori_loop(*self.offsets, go, 0)
+        if self.own is not None:
+            self.own().start()
+        self.flights.append(self)
+        return self
+
+    def arrive(self):
+        self.whole().wait_recv()
+        if self.own is not None:
+            self.own().wait()
+        self.arrived = True
+
+    def leave(self):
+        self.whole().wait_send()
+        self.left = True
+
+    def land(self):
+        if not self.arrived:
+            self.arrive()
+        if not self.left:
+            self.leave()
+
+
+class Reduce:
+    def __init__(self, flights, place, blocks, bits, landing, kept, send, recv, last):
+        self.flights, self.place = flights, place
+        self.blocks, self.bits, self.last = blocks, bits, last
+        self.landing, self.kept, self.send, self.recv = landing, kept, send, recv
+        self.rows = blocks.shape[2]
+        self.parts = send.shape[1]
+        self.under_way = {}
+
+    def cut(self, part):
+        size = self.rows // self.parts
+        return pl.ds(part * size, size)
+
+    def copy(self, stage, part):
+        place, rows = self.place, self.cut(part)
+        if stage == 0:
+            source = self.blocks.at[:, 1 - place.core, rows, :]
+            target = place.other_core
+        else:
+            count = self.blocks.shape[0] >> stage
+            bit = self.bits[stage - 1]
+            source = self.kept[stage - 1].at[
+                pl.ds((1 - place.bit(bit)) * count, count), rows, :
+            ]
+            target = place.across(bit)
+        return pltpu.make_async_remote_copy(
+            src_ref=source,
+            dst_ref=self.landing[stage].at[:, rows, :],
+            send_sem=self.send.at[stage, part],
+            recv_sem=self.recv.at[stage, part],
+            device_id=target,
+            device_id_type=MESH,
+        )
+
+    def start(self, stage, part):
+        copy = functools.partial(self.copy, stage, part)
+        self.under_way[stage, part] = Flight(self.flights, copy).start()
+
+    def step(self, stage, part):
+        self.finish(stage, part)
+        if stage < len(self.bits):
+            self.start(stage + 1, part)
+
+    def finish(self, stage, part):
+        place, rows = self.place, self.cut(part)
+        self.under_way[stage, part].arrive()
+        count = self.blocks.shape[0] >> stage
+        if stage == 0:
+            own = self.blocks[:, place.core, rows, :]
+        else:
+            first = place.bit(self.bits[stage - 1]) * count
+            own = self.kept[stage - 1][pl.ds(first, count), rows, :]
+        landed = self.landing[stage][:, rows, :]
+        if stage < len(self.bits):
+            self.kept[stage][:, rows, :] = own + landed
+        else:
+            self.last(rows, own.astype(jnp.float32) + landed.astype(jnp.float32))
+
+
+class Place:
+    def __init__(self, ranks):
+        self.ranks = ranks
+        self.rank = lax.axis_index("wide")
+        self.core = lax.axis_index("rep")
+        self.other_core = (self.rank, 1 - self.core)
+
+    def bit(self, index):
+        return (self.rank // (1 << index)) % 2
+
+    def across(self, index):
+        step = 1 << index
+        return (self.rank + step - 2 * step * self.bit(index), self.core)
+
+
+def block_order(ranks, order):
+    places = []
+    for rank in range(ranks):
+        spot = 0
+        for bit in order:
+            spot = spot * 2 + (rank >> bit) % 2
+        places.append(spot)
+    return places
+
+
+def fused_kernel(names, spans, ranks, table_rows, *refs):
+    s = types.SimpleNamespace(**dict(zip(names, refs, strict=True)))
+    place = Place(ranks)
+    bits = (ranks - 1).bit_length()
+    far = list(range(2, bits))
+    images_here, pixels, channels = s.arrived.shape
+    every_image = range(images_here)
+    flat_rows = images_here * pixels
+    piece = pixels // ranks
+    half = channels // 2
+    steps = pixels // CHUNK
+    score_scale = channels ** (-0.5)
+    count_inverse = 1.0 / (pixels * (channels // GROUPS))
+    col = lax.broadcasted_iota(jnp.int32, (CHUNK, 1), 0) % SIDE
+    flights = []
+
+    def image_rows(image):
+        return slice(image * pixels, (image + 1) * pixels)
+
+    barrier = pltpu.get_barrier_semaphore()
+
+    def greet(offset, carry):
+        pl.semaphore_signal(
+            barrier,
+            inc=1,
+            device_id=((place.rank + offset) % ranks, place.core),
+            device_id_type=MESH,
+        )
+        return carry
+
+    lax.fori_loop(1, ranks, greet, 0)
+    pl.semaphore_signal(barrier, inc=1, device_id=place.other_core, device_id_type=MESH)
+
+    pairs = (
+        (s.noise_table, s.noise_table_here.at[pl.ds(0, table_rows), :]),
+        (s.embed_weight, s.embed_weight_here),
+        (s.conv_one, s.conv_one_here),
+        (s.conv_two, s.conv_two_here),
+        (s.query_weight, s.query_weight_here),
+        (s.key_weight, s.key_weight_here),
+        (s.value_weight, s.value_weight_here),
+        (s.out_weight, s.out_weight_here),
+    )
+    loads = []
+    for index, (source, target) in enumerate(pairs):
+        loads.append(pltpu.make_async_copy(source, target, s.load_sem.at[index]))
+        loads[-1].start()
+    pl.semaphore_wait(barrier, ranks)
+
+    def gather_copy(slot, source, target, image, offset):
+        peer = (place.rank + offset) % ranks
+        return pltpu.make_async_remote_copy(
+            src_ref=source.at[peer * images_here + image],
+            dst_ref=target.at[image, pl.ds(pl.multiple_of(place.rank * piece, 16), piece)],
+            send_sem=s.swap_send.at[slot],
+            recv_sem=s.swap_recv.at[slot],
+            device_id=(peer, place.core),
+            device_id_type=MESH,
+        )
+
+    def gather_own(slot, source, target, image):
+        return pltpu.make_async_copy(
+            source.at[place.rank * images_here + image],
+            target.at[image, pl.ds(pl.multiple_of(place.rank * piece, 16), piece)],
+            s.swap_own.at[slot],
+        )
+
+    def scatter_copy(slot, source, target, image, offset):
+        peer = (place.rank + offset) % ranks
+        return pltpu.make_async_remote_copy(
+            src_ref=source.at[image, pl.ds(pl.multiple_of(peer * piece, 16), piece)],
+            dst_ref=target.at[place.rank * images_here + image],
+            send_sem=s.swap_send.at[slot],
+            recv_sem=s.swap_recv.at[slot],
+            device_id=(peer, place.core),
+            device_id_type=MESH,
+        )
+
+    def scatter_own(slot, source, target, image):
+        return pltpu.make_async_copy(
+            source.at[image, pl.ds(pl.multiple_of(place.rank * piece, 16), piece)],
+            target.at[place.rank * images_here + image],
+            s.swap_own.at[slot],
+        )
+
+    def swap_whole(slot, held, image):
+        others = held.at[image, pl.ds(0, pixels - piece)]
+        return pltpu.make_async_remote_copy(
+            src_ref=others,
+            dst_ref=others,
+            send_sem=s.swap_send.at[slot],
+            recv_sem=s.swap_recv.at[slot],
+            device_id=place.across(0),
+            device_id_type=MESH,
+        )
+
+    def swaps(copy, own, which, source, target, held):
+        return [
+            Flight(
+                flights,
+                functools.partial(copy, which * images_here + image, source, target, image),
+                (1, ranks),
+                functools.partial(swap_whole, which * images_here + image, held, image),
+                functools.partial(own, which * images_here + image, source, target, image),
+            )
+            for image in every_image
+        ]
+
+    swap_images = swaps(gather_copy, gather_own, 0, s.images, s.arrived, s.arrived)
+    swap_upstream = swaps(gather_copy, gather_own, 1, s.cotangent, s.upstream, s.upstream)
+    swap_output = swaps(scatter_copy, scatter_own, 2, s.leaving, s.output, s.leaving)
+    swap_grad = swaps(scatter_copy, scatter_own, 3, s.leaving_grad, s.input_grad, s.leaving_grad)
+    for image in every_image:
+        swap_images[image].start()
+
+    for padded in (s.spread_act, s.spread_two, s.spread_one, s.spread_far):
+        for image in every_image:
+            edge = jnp.zeros((SIDE, padded.shape[2]), jnp.bfloat16)
+            padded[image, 0:SIDE, :] = edge
+            padded[image, pixels + SIDE : pixels + 2 * SIDE, :] = edge
+    tail = s.noise_table_here.shape[0] - table_rows
+    if tail:
+        s.noise_table_here[table_rows:, :] = jnp.zeros((tail, channels), jnp.bfloat16)
+    own_levels = [s.levels[place.rank * images_here + image] for image in every_image]
+    entry = lax.broadcasted_iota(jnp.int32, (8, s.noise_table_here.shape[0]), 1)
+    line = lax.broadcasted_iota(jnp.int32, entry.shape, 0)
+    selected = jnp.zeros(entry.shape, jnp.float32)
+    for image in every_image:
+        hit = jnp.where(entry == own_levels[image], 1.0, 0.0)
+        selected = jnp.where(line == image, hit, selected)
+    loads[0].wait()
+    loads[1].wait()
+    embedded = matmul(selected.astype(jnp.bfloat16), s.noise_table_here[...])
+    embed_shift = matmul(embedded.astype(jnp.bfloat16), s.embed_weight_here[...])
+    embed_shift = embed_shift + s.embed_bias[...] + s.bias_one[...]
+
+    def over(image, body, start):
+        return lax.fori_loop(0, steps, functools.partial(body, image), start)
+
+    def at(step):
+        return pl.ds(pl.multiple_of(step * CHUNK, CHUNK), CHUNK)
+
+    def flat_at(image, step):
+        return pl.ds(pl.multiple_of(image * pixels + step * CHUNK, CHUNK), CHUNK)
+
+    def fold(chunk):
+        return jnp.sum(chunk.reshape(CHUNK // 8, 8, channels), axis=0)
+
+    none = jnp.zeros((8, channels), jnp.float32)
+
+    def whole(part):
+        return jnp.sum(part, axis=0, keepdims=True)
+
+    group_width = s.same_group.shape[0]
+    same_group = [
+        lax.broadcasted_iota(jnp.int32, (group_width, group_width), axis)
+        // (channels // GROUPS)
+        for axis in range(2)
+    ]
+    s.same_group[...] = jnp.where(same_group[0] == same_group[1], 1.0, 0.0).astype(jnp.bfloat16)
+
+    def group_total(row):
+        rows = jnp.broadcast_to(row, (8, channels))
+        return group_sum(rows, s.same_group[...])[0:1] * count_inverse
+
+    def statistics(load, image):
+        def first(image, step, total):
+            return total + fold(load(image, step))
+
+        center = group_total(whole(over(image, first, none)))
+
+        def second(image, step, total):
+            spread = load(image, step) - center
+            return total + fold(spread * spread)
+
+        variance = group_total(whole(over(image, second, none)))
+        return center, lax.rsqrt(variance + epsilon)
+
+    def spread_out(target, image, step, chunk, before, after):
+        width = chunk.shape[1]
+        rows = pl.ds(pl.multiple_of(step * CHUNK + SIDE, SIDE), CHUNK)
+        target[image, rows, before * width : (before + 1) * width] = jnp.where(
+            col > 0, pltpu.roll(chunk, 1, 0), 0.0
+        ).astype(jnp.bfloat16)
+        target[image, rows, width : 2 * width] = chunk.astype(jnp.bfloat16)
+        target[image, rows, after * width : (after + 1) * width] = jnp.where(
+            col < SIDE - 1, pltpu.roll(chunk, CHUNK - 1, 0), 0.0
+        ).astype(jnp.bfloat16)
+
+    def activate(load, image, moments, gain, shift, keep):
+        center, rate = moments
+        slope = rate * gain
+
+        def apply(image, step, carry):
+            field = (load(image, step) - center) * slope + shift
+            act = field * sigmoid(field)
+            spread_out(s.spread_act, image, step, act, 0, 2)
+            keep[flat_at(image, step), :] = act.astype(jnp.bfloat16)
+            return carry
+
+        over(image, apply, 0)
+
+    def convolve(weight, image):
+        total = None
+        for row_tap in range(3):
+            term = matmul(
+                s.spread_act[image, SIDE * row_tap : SIDE * row_tap + pixels, :],
+                weight[3 * channels * row_tap : 3 * channels * (row_tap + 1), :],
+            )
+            total = term if total is None else total + term
+        return total
+
+    def tap_rows(row_tap):
+        return slice(SIDE * (2 - row_tap), SIDE * (2 - row_tap) + pixels)
+
+    def convolve_back(source, weight, images):
+        total = None
+        for tap in range(9):
+            window = source[
+                images, tap_rows(tap // 3), (tap % 3) * channels : (tap % 3 + 1) * channels
+            ]
+            term = against(
+                window.reshape(-1, channels), weight[channels * tap : channels * (tap + 1), :]
+            )
+            total = term if total is None else total + term
+        return total
+
+    def share_copy(slot, source, target, bit):
+        def make():
+            return pltpu.make_async_remote_copy(
+                src_ref=source,
+                dst_ref=target,
+                send_sem=s.share_send.at[slot],
+                recv_sem=s.share_recv.at[slot],
+                device_id=place.across(bit),
+                device_id_type=MESH,
+            )
+
+        return Flight(flights, make)
+
+    bit_one, bit_two = 1, 0
+    half_one, half_two = place.bit(bit_one), place.bit(bit_two)
+
+    def shares(which, source, target, bit, mine=None):
+        made = []
+        for image in every_image:
+            rows = pl.ds(image * pixels, pixels)
+            lanes_sent = pl.ds(0, channels)
+            if mine is not None:
+                lanes_sent = pl.ds(pl.multiple_of((1 - mine) * half, half), half)
+            made.append(
+                share_copy(
+                    which * images_here + image,
+                    source.at[rows, lanes_sent],
+                    target.at[rows, :],
+                    bit,
+                )
+            )
+        return made
+
+    share_act_one = shares(0, s.act_one, s.act_one_far, bit_one)
+    share_act_two = shares(1, s.act_two, s.act_two_far, bit_two)
+    share_grad_two = shares(2, s.grad_two, s.grad_two_far, bit_two, half_two)
+    share_grad_one = shares(3, s.grad_one, s.grad_one_far, bit_one, half_one)
+
+    def weigh(spread, mine, act, act_far, grad_far, blocks, spots):
+        def unfold(image, step, carry):
+            chunk = grad_far[flat_at(image, step), :].astype(jnp.float32)
+            spread_out(s.spread_far, image, step, chunk, 2, 0)
+            return carry
+
+        for image in every_image:
+            over(image, unfold, 0)
+        rows_block = blocks.shape[2]
+        for tap in range(9):
+            rows, side_tap = tap_rows(tap // 3), tap % 3
+            near = spread[
+                :, rows, pl.ds(pl.multiple_of(side_tap * channels + mine * half, half), half)
+            ]
+            beyond = s.spread_far[:, rows, side_tap * half : (side_tap + 1) * half]
+            product = by_rows(act[...], near.reshape(flat_rows, half)) + by_rows(
+                act_far[...], beyond.reshape(flat_rows, half)
+            )
+            product = product.astype(jnp.bfloat16)
+            done = 0
+            while done < channels:
+                block, inside = divmod(tap * channels + done, rows_block)
+                size = min(rows_block - inside, channels - done)
+                blocks[spots[block // 2], block % 2, inside : inside + size, :] = product[
+                    done : done + size
+                ]
+                done = done + size
+
+    order_one = [1 - bit_one] + far
+    order_two = [1 - bit_two] + far
+    order_mix = [0, 1] + far
+    spots_one = block_order(ranks, order_one + [bit_one])
+    spots_two = block_order(ranks, order_two + [bit_two])
+    spots_mix = block_order(ranks, order_mix)
+
+    def put_one(rows, total):
+        s.sum_one[:, rows, :] = total
+        s.fin_one[:, rows, :] = total.astype(jnp.bfloat16)
+
+    def put_two(rows, total):
+        s.sum_two[:, rows, :] = total
+        s.fin_two[:, rows, :] = total.astype(jnp.bfloat16)
+
+    def put_mix(rows, total):
+        s.share_mix[rows, :] = total[0]
+
+    def staged(ref, first, stages):
+        views, start = [], 0
+        for stage in range(stages):
+            views.append(ref.at[pl.ds(start, first >> stage)])
+            start = start + (first >> stage)
+        return views
+
+    def reduction(blocks, order, landing, kept, send, recv, put):
+        stages = len(order)
+        return Reduce(
+            flights,
+            place,
+            blocks,
+            order,
+            staged(landing, ranks, stages + 1),
+            staged(kept, ranks, stages),
+            send,
+            recv,
+            put,
+        )
+
+    reduce_one = reduction(
+        s.blocks_one,
+        order_one,
+        s.land_one,
+        s.kept_one,
+        s.reduce_send_one,
+        s.reduce_recv_one,
+        put_one,
+    )
+    reduce_two = reduction(
+        s.blocks_two,
+        order_two,
+        s.land_two,
+        s.kept_two,
+        s.reduce_send_two,
+        s.reduce_recv_two,
+        put_two,
+    )
+    reduce_mix = reduction(
+        s.blocks_mix,
+        order_mix,
+        s.land_mix,
+        s.kept_mix,
+        s.reduce_send_mix,
+        s.reduce_recv_mix,
+        put_mix,
+    )
+    parts = reduce_one.parts
+
+    def settle(flight, sums, target, mine):
+        flight.arrive()
+        own = sums[mine]
+        other = target[...].astype(jnp.float32)
+        left = jnp.where(mine == 0, own, other)
+        right = jnp.where(mine == 0, other, own)
+        return jnp.concatenate([left, right], axis=1)
+
+    def small_copy(stage):
+        return pltpu.make_async_remote_copy(
+            src_ref=s.small_sum.at[stage],
+            dst_ref=s.small_land.at[stage],
+            send_sem=s.small_send.at[stage],
+            recv_sem=s.small_recv.at[stage],
+            device_id=place.other_core if stage == 0 else place.across(stage - 1),
+            device_id_type=MESH,
+        )
+
+    small = [Flight(flights, functools.partial(small_copy, k)) for k in range(bits + 1)]
+
+    def small_step(stage):
+        small[stage].arrive()
+        s.small_sum[stage + 1] = s.small_sum[stage] + s.small_land[stage]
+        if stage < bits:
+            small[stage + 1].start()
+
+    slot_rows = 16
+    lanes = s.slots.shape[1]
+
+    def pair_window():
+        return s.slots.at[pl.ds(pl.multiple_of(place.rank * 2 * slot_rows, 16), 2 * slot_rows), :]
+
+    def slot_copy():
+        first = pl.multiple_of((place.rank * 2 + place.core) * slot_rows, slot_rows)
+        window = s.slots.at[pl.ds(first, slot_rows), :]
+        return pltpu.make_async_remote_copy(
+            src_ref=window,
+            dst_ref=window,
+            send_sem=s.slots_send.at[0],
+            recv_sem=s.slots_recv.at[0],
+            device_id=place.other_core,
+            device_id_type=MESH,
+        )
+
+    def pair_copy(offset):
+        return pltpu.make_async_remote_copy(
+            src_ref=pair_window(),
+            dst_ref=pair_window(),
+            send_sem=s.slots_send.at[1],
+            recv_sem=s.slots_recv.at[1],
+            device_id=((place.rank + offset) % ranks, place.core),
+            device_id_type=MESH,
+        )
+
+    slots_pair = Flight(flights, slot_copy)
+    def pairs_whole():
+        others = s.slots.at[pl.ds(0, (ranks - 1) * 2 * slot_rows), :]
+        return pltpu.make_async_remote_copy(
+            src_ref=others,
+            dst_ref=others,
+            send_sem=s.slots_send.at[1],
+            recv_sem=s.slots_recv.at[1],
+            device_id=place.across(0),
+            device_id_type=MESH,
+        )
+
+    slots_all = Flight(flights, pair_copy, (1, ranks), pairs_whole)
+
+    def load_input(image, step):
+        return s.arrived[image, at(step), :].astype(jnp.float32)
+
+    def load_hidden(image, step):
+        return s.hidden[flat_at(image, step), :]
+
+    def load_middle(image, step):
+        return s.middle[flat_at(image, step), :]
+
+    def load_upstream(image, step):
+        return s.upstream[image, at(step), :].astype(jnp.float32)
+
+    def delta_at(image, step):
+        return s.delta[flat_at(image, step), :]
+
+    def load_low(ref):
+        return lambda image, step: ref[flat_at(image, step), :].astype(jnp.float32)
+
+    gain_one, shift_one = s.gain_one[...], s.shift_one[...]
+    gain_two, shift_two = s.gain_two[...], s.shift_two[...]
+    gain_three, shift_three = s.gain_three[...], s.shift_three[...]
+    moments_one, moments_two, moments_three = [], [], []
+    sums = {name: [] for name in SUMS}
+
+    def forward(image):
+        rows = image_rows(image)
+        swap_images[image].arrive()
+        if image == images_here - 1:
+            for later in every_image:
+                swap_upstream[later].start()
+        moments_one.append(statistics(load_input, image))
+        activate(load_input, image, moments_one[image], gain_one, shift_one, s.act_one)
+        share_act_one[image].start()
+        if image == 0:
+            loads[2].wait()
+        s.hidden[rows, :] = convolve(s.conv_one_here, image) + embed_shift[image : image + 1]
+        moments_two.append(statistics(load_hidden, image))
+        activate(load_hidden, image, moments_two[image], gain_two, shift_two, s.act_two)
+        share_act_two[image].start()
+        if image == 0:
+            loads[3].wait()
+        s.middle[rows, :] = (
+            convolve(s.conv_two_here, image)
+            + s.bias_two[...]
+            + s.arrived[image].astype(jnp.float32)
+        )
+        moments_three.append(statistics(load_middle, image))
+        center, rate = moments_three[image]
+        slope = rate * gain_three
+
+        def normalize(image, step, carry):
+            field = (load_middle(image, step) - center) * slope + shift_three
+            s.normed[flat_at(image, step), :] = field.astype(jnp.bfloat16)
+            return carry
+
+        over(image, normalize, 0)
+        if image == 0:
+            for load in loads[4:]:
+                load.wait()
+        normed = s.normed[rows, :]
+        query = (matmul(normed, s.query_weight_here[...]) + s.query_bias[...]).astype(jnp.bfloat16)
+        key = matmul(normed, s.key_weight_here[...]).astype(jnp.bfloat16)
+        value = (matmul(normed, s.value_weight_here[...]) + s.value_bias[...]).astype(jnp.bfloat16)
+        s.query[rows, :] = query
+        s.key[rows, :] = key
+        s.value[rows, :] = value
+        scores = against(query, key) * score_scale
+        exponent = jnp.exp(scores - jnp.max(scores, axis=1, keepdims=True))
+        probs = exponent / jnp.sum(exponent, axis=1, keepdims=True)
+        s.probs[rows, :] = probs
+        mixed = matmul(probs.astype(jnp.bfloat16), value).astype(jnp.bfloat16)
+        s.mixed[rows, :] = mixed
+        result = s.middle[rows, :] + matmul(mixed, s.out_weight_here[...]) + s.out_bias[...]
+        s.leaving[image] = result.astype(jnp.bfloat16)
+
+    def norm_back_terms(gain, shift_sum, gain_sum):
+        rows = stack_rows([gain * shift_sum, gain * gain_sum])
+        means = group_sum(rows, s.same_group[...]) * count_inverse
+        return means[0:1], means[1:2]
+
+    def backward(image):
+        rows = image_rows(image)
+        swap_upstream[image].arrive()
+        probs = s.probs[rows, :]
+        query, key, value = s.query[rows, :], s.key[rows, :], s.value[rows, :]
+        grad_mixed = against(s.upstream[image], s.out_weight_here[...]).astype(jnp.bfloat16)
+        grad_probs = against(grad_mixed, value)
+        grad_value = by_rows(probs.astype(jnp.bfloat16), grad_mixed).astype(jnp.bfloat16)
+        inner = jnp.sum(grad_probs * probs, axis=1, keepdims=True)
+        grad_scores = (probs * (grad_probs - inner)).astype(jnp.bfloat16)
+        grad_query = (matmul(grad_scores, key) * score_scale).astype(jnp.bfloat16)
+        grad_key = (by_rows(grad_scores, query) * score_scale).astype(jnp.bfloat16)
+        s.grad_value[rows, :] = grad_value
+        s.grad_query[rows, :] = grad_query
+        s.grad_key[rows, :] = grad_key
+        s.delta[rows, :] = (
+            against(grad_query, s.query_weight_here[...])
+            + against(grad_key, s.key_weight_here[...])
+            + against(grad_value, s.value_weight_here[...])
+        )
+
+        center, rate = moments_three[image]
+
+        def sums_three(image, step, totals):
+            grad = delta_at(image, step)
+            unit = (load_middle(image, step) - center) * rate
+            return totals[0] + fold(grad), totals[1] + fold(grad * unit)
+
+        shift_sum, gain_sum = map(whole, over(image, sums_three, (none, none)))
+        sums["gain_three"].append(gain_sum)
+        sums["shift_three"].append(shift_sum)
+        mean_shift, mean_gain = norm_back_terms(gain_three, shift_sum, gain_sum)
+
+        def back_three(image, step, total):
+            unit = (load_middle(image, step) - center) * rate
+            grad = rate * (delta_at(image, step) * gain_three - mean_shift - unit * mean_gain)
+            grad = grad + load_upstream(image, step)
+            s.grad_middle[flat_at(image, step), :] = grad
+            low = grad.astype(jnp.bfloat16)
+            s.grad_two[flat_at(image, step), :] = low
+            low = low.astype(jnp.float32)
+            spread_out(s.spread_two, image, step, low, 2, 0)
+            return total + fold(low)
+
+        sums["bias_two"].append(whole(over(image, back_three, none)))
+        share_grad_two[image].start()
+
+        s.delta[rows, :] = convolve_back(s.spread_two, s.conv_two_here, slice(image, image + 1))
+
+        def put_hidden(image, step, grad, total):
+            low = grad.astype(jnp.bfloat16)
+            s.grad_one[flat_at(image, step), :] = low
+            low = low.astype(jnp.float32)
+            spread_out(s.spread_one, image, step, low, 2, 0)
+            return total + fold(low)
+
+        gain_sum, shift_sum, total = swish_norm_back(
+            load_hidden, image, moments_two[image], gain_two, shift_two, put_hidden, none
+        )
+        share_grad_one[image].start()
+        sums["gain_two"].append(gain_sum)
+        sums["shift_two"].append(shift_sum)
+        sums["bias_one"].append(whole(total))
+
+    def swish_norm_back(load, image, moments, gain, shift, put, start):
+        center, rate = moments
+
+        def totals(image, step, carry):
+            unit = (load(image, step) - center) * rate
+            field = unit * gain + shift
+            gate = sigmoid(field)
+            grad = delta_at(image, step) * (gate * (1.0 + field * (1.0 - gate)))
+            s.delta[flat_at(image, step), :] = grad
+            return carry[0] + fold(grad), carry[1] + fold(grad * unit)
+
+        shift_sum, gain_sum = map(whole, over(image, totals, (none, none)))
+        mean_shift, mean_gain = norm_back_terms(gain, shift_sum, gain_sum)
+
+        def back(image, step, carry):
+            unit = (load(image, step) - center) * rate
+            grad = rate * (delta_at(image, step) * gain - mean_shift - unit * mean_gain)
+            return put(image, step, grad, carry)
+
+        return gain_sum, shift_sum, over(image, back, start)
+
+    def backward_input(image):
+        def put_input(image, step, grad, carry):
+            total = grad + s.grad_middle[flat_at(image, step), :]
+            s.leaving_grad[image, at(step), :] = total.astype(jnp.bfloat16)
+            return carry
+
+        gain_sum, shift_sum, _ = swish_norm_back(
+            load_input, image, moments_one[image], gain_one, shift_one, put_input, 0
+        )
+        swap_grad[image].start()
+        sums["gain_one"].append(gain_sum)
+        sums["shift_one"].append(shift_sum)
+
+    mix_rows = s.blocks_mix.shape[2] // 4
+
+    def store_mix(which, product):
+        product = product.astype(jnp.bfloat16)
+        for rank in range(ranks):
+            for core in range(2):
+                block = rank * 2 + core
+                s.blocks_mix[
+                    spots_mix[rank], core, which * mix_rows : (which + 1) * mix_rows, :
+                ] = product[block * mix_rows : (block + 1) * mix_rows]
+
+    def weigh_mix():
+        upstream = s.upstream[...].reshape(flat_rows, channels)
+        normed = s.normed[...]
+        store_mix(3, by_rows(s.mixed[...], upstream))
+        store_mix(0, by_rows(normed, s.grad_query[...]))
+        store_mix(1, by_rows(normed, s.grad_key[...]))
+        store_mix(2, by_rows(normed, s.grad_value[...]))
+
+    def column_sums(load):
+        def body(image, step, total):
+            return total + fold(load(image, step))
+
+        total = none
+        for image in every_image:
+            total = over(image, body, total)
+        return whole(total)
+
+    def fill_slot():
+        slot_place = lax.broadcasted_iota(jnp.int32, (slot_rows, lanes), 0)
+        slot = jnp.zeros((slot_rows, lanes), jnp.float32)
+        for image in every_image:
+            for index in range(per_image):
+                row = sums["bias_one"][image][:, index * lanes : (index + 1) * lanes]
+                slot = jnp.where(
+                    slot_place == image * per_image + index,
+                    jnp.broadcast_to(row, slot.shape),
+                    slot,
+                )
+            slot = jnp.where(
+                slot_place == images_here * per_image + image,
+                own_levels[image].astype(jnp.float32),
+                slot,
+            )
+        device = place.rank * 2 + place.core
+        s.slots[pl.ds(pl.multiple_of(device * slot_rows, slot_rows), slot_rows), :] = slot
+
+    per_image = channels // lanes
+
+    def flat(first, rows):
+        count, width = rows.shape[0], rows.shape[1] // lanes
+        for index in range(width):
+            s.flat[pl.ds(first + index, count, stride=width), :] = rows[
+                :, index * lanes : (index + 1) * lanes
+            ]
+
+    def embedding_gradients():
+        def every(index):
+            return s.slots[pl.ds(index, ranks * 2, stride=slot_rows), :]
+
+        device = place.rank * 2 + place.core
+        de = jnp.concatenate(
+            [
+                jnp.concatenate([every(image * per_image + j) for j in range(per_image)], axis=1)
+                for image in every_image
+            ],
+            axis=0,
+        )
+        levels = jnp.concatenate(
+            [every(images_here * per_image + image) for image in every_image], axis=0
+        ).astype(jnp.int32)[:, 0:1]
+        entry = lax.broadcasted_iota(
+            jnp.int32, (levels.shape[0], s.noise_table_here.shape[0]), 1
+        )
+        hit = jnp.where(entry == levels, 1.0, 0.0).astype(jnp.bfloat16)
+        everywhere = matmul(hit, s.noise_table_here[...])
+        exact = dict(preferred_element_type=jnp.float32, precision=lax.Precision.HIGHEST)
+        own_rows = channels // (ranks * 2)
+        s.product[...] = lax.dot_general(everywhere, de, (((0,), (0,)), ((), ())), **exact)
+        first = pl.multiple_of(device * own_rows, own_rows)
+        flat(spans["embed"], s.product[pl.ds(first, own_rows), :])
+        grad_rows = lax.dot_general(
+            de, s.embed_weight_here[...].astype(jnp.float32), (((1,), (1,)), ((), ())), **exact
+        )
+        halves = table_rows * 2 // (ranks * 2)
+        wide = -(-halves // 128) * 128
+        spot = lax.broadcasted_iota(jnp.int32, (levels.shape[0], wide), 1) + device * halves
+        total = jnp.zeros((wide, half), jnp.float32)
+        for side in range(2):
+            pick = jnp.where(2 * levels + side == spot, 1.0, 0.0)
+            total = total + lax.dot_general(
+                pick,
+                grad_rows[:, side * half : (side + 1) * half],
+                (((0,), (0,)), ((), ())),
+                **exact,
+            )
+        flat(spans["table"], total)
+
+    def start_small():
+        sums["query_bias"].append(column_sums(load_low(s.grad_query)))
+        sums["value_bias"].append(column_sums(load_low(s.grad_value)))
+        sums["out_bias"].append(column_sums(load_upstream))
+        rows = [functools.reduce(jnp.add, sums[name]) for name in SUMS]
+        s.small_sum[0, 0:8, :] = stack_rows(rows[:8])
+        s.small_sum[0, 8:16, :] = stack_rows(rows[8:])
+        small[0].start()
+
+    def step_all(reduction, stage):
+        for part in range(reduction.parts):
+            reduction.step(stage, part)
+
+    for image in every_image:
+        forward(image)
+    backward(0)
+    for image in every_image[1:]:
+        backward(image)
+    for image in every_image:
+        swap_output[image].start()
+    fill_slot()
+    slots_pair.start()
+    weigh_mix()
+    reduce_mix.start(0, 0)
+    slots_pair.arrive()
+    slots_all.start()
+    for image in every_image:
+        share_act_two[image].arrive()
+        share_grad_two[image].arrive()
+    weigh(
+        s.spread_two, half_two, s.act_two, s.act_two_far, s.grad_two_far, s.blocks_two, spots_two
+    )
+    for part in range(parts):
+        reduce_two.start(0, part)
+    reduce_mix.step(0, 0)
+    s.delta[...] = convolve_back(s.spread_one, s.conv_one_here, slice(None))
+    for image in every_image:
+        backward_input(image)
+    start_small()
+    step_all(reduce_two, 0)
+    for image in every_image:
+        share_act_one[image].arrive()
+        share_grad_one[image].arrive()
+    weigh(
+        s.spread_one, half_one, s.act_one, s.act_one_far, s.grad_one_far, s.blocks_one, spots_one
+    )
+    for part in range(parts):
+        reduce_one.start(0, part)
+    small_step(0)
+    step_all(reduce_one, 0)
+    slots_all.arrive()
+    embedding_gradients()
+    reduce_mix.step(1, 0)
+    small_step(1)
+
+    reduce_two.step(1, 0)
+    reduce_one.step(1, 0)
+    reduce_two.step(1, 1)
+    reduce_two.step(2, 0)
+    reduce_mix.step(2, 0)
+    small_step(2)
+    reduce_one.step(1, 1)
+    reduce_one.step(2, 0)
+    reduce_two.step(1, 2)
+    reduce_two.step(2, 1)
+    reduce_two.step(3, 0)
+    reduce_mix.step(3, 0)
+    small_step(3)
+    reduce_one.step(1, 2)
+    reduce_one.step(2, 1)
+    reduce_one.step(3, 0)
+    reduce_two.step(2, 2)
+    reduce_two.step(3, 1)
+    reduce_mix.step(4, 0)
+    small_step(4)
+    s.sums[...] = s.small_sum[bits + 1]
+    for index, name in enumerate(dict(query=0, key=0, value=0, out=0)):
+        flat(spans[name], s.share_mix[index * mix_rows : (index + 1) * mix_rows, :])
+    reduce_one.step(2, 2)
+    reduce_one.step(3, 1)
+    reduce_two.step(3, 2)
+    end_two = share_copy(4 * images_here, s.fin_two.at[1 - half_two], s.last_two, bit_two).start()
+    reduce_one.step(3, 2)
+    end_one = share_copy(
+        4 * images_here + 1, s.fin_one.at[1 - half_one], s.last_one, bit_one
+    ).start()
+    flat(spans["conv_two"], settle(end_two, s.sum_two, s.last_two, half_two))
+    flat(spans["conv_one"], settle(end_one, s.sum_one, s.last_one, half_one))
+
+    for flight in flights:
+        flight.land()
+
+
+def last_kernel(starts, rows, *refs):
+    output_in, grad_in, flat_in, sums_in, output, grad = refs[:6]
+    flats, sums = refs[6 : 6 + len(starts)], refs[6 + len(starts) : -4]
+    output_here, grad_here, flat_here, sems = refs[-4:]
+    arrive = [
+        pltpu.make_async_copy(output_in, output_here, sems.at[0]),
+        pltpu.make_async_copy(grad_in, grad_here, sems.at[1]),
+        pltpu.make_async_copy(flat_in, flat_here, sems.at[2]),
+    ]
+    for move in arrive:
+        move.start()
+    for row, target in zip(rows, sums, strict=True):
+        target[...] = sums_in[row : row + 1, :]
+    leave = [
+        pltpu.make_async_copy(output_here, output, sems.at[3]),
+        pltpu.make_async_copy(grad_here, grad, sems.at[4]),
+    ]
+    for index, (start, target) in enumerate(zip(starts, flats, strict=True)):
+        span = flat_here.at[pl.ds(start, target.shape[0]), :]
+        leave.append(pltpu.make_async_copy(span, target, sems.at[5 + index]))
+    for index, move in enumerate(arrive):
+        move.wait()
+        for out in leave[index : index + 1] if index < 2 else leave[2:]:
+            out.start()
+    for move in leave:
+        move.wait()
+
+
+def fused_device(given):
+    ranks = lax.axis_size("wide")
+    bits = (ranks - 1).bit_length()
+    images = given["images"]
+    images_rep, piece, channels = images.shape
+    images_here, pixels = images_rep // ranks, piece * ranks
+    flat_rows = images_here * pixels
+    half = channels // 2
+    devices = ranks * 2
+    table_rows = given["noise_table"].shape[0]
+    padded_rows = -(-table_rows // 128) * 128
+    conv_rows = given["conv_one"].shape[0] // devices
+    mix_rows = 4 * channels // devices
+    low, full = jnp.bfloat16, jnp.float32
+    parts = 3
+    lanes = 128
+
+    def struct(shape, kind):
+        return jax.ShapeDtypeStruct(shape, kind)
+
+    def hold(*shape, kind=low):
+        return pltpu.VMEM(shape, kind)
+
+    def semaphores(*shape):
+        return pltpu.SemaphoreType.DMA(shape)
+
+    def activations():
+        return hold(flat_rows, channels)
+
+    def fields():
+        return hold(flat_rows, channels, kind=full)
+
+    def square():
+        return hold(channels, channels)
+
+    def images_low():
+        return hold(images_here, pixels, channels)
+
+    def flat_span(size, pad=False):
+        rows = size // lanes
+        return -(-rows // 128) * 128 if pad else rows
+
+    share = channels * channels // devices
+    sizes = dict(
+        conv_one=flat_span(conv_rows * channels),
+        conv_two=flat_span(conv_rows * channels),
+        query=flat_span(share),
+        key=flat_span(share),
+        value=flat_span(share),
+        out=flat_span(share),
+        embed=flat_span(share),
+        table=flat_span(table_rows * channels // devices, True),
+    )
+    spans, start = {}, 0
+    for name, size in sizes.items():
+        spans[name] = start
+        start = start + size
+
+    outputs = dict(
+        output=struct(images.shape, low),
+        input_grad=struct(images.shape, low),
+        flat=struct((start, lanes), full),
+        sums=struct((16, channels), full),
+    )
+    padded = pixels + 2 * SIDE
+    halvings = sum(ranks >> stage for stage in range(bits + 1))
+    scratch = dict(
+        noise_table_here=hold(padded_rows, channels),
+        embed_weight_here=square(),
+        conv_one_here=hold(*given["conv_one"].shape),
+        conv_two_here=hold(*given["conv_two"].shape),
+        query_weight_here=square(),
+        key_weight_here=square(),
+        value_weight_here=square(),
+        out_weight_here=square(),
+        arrived=images_low(),
+        upstream=images_low(),
+        leaving=images_low(),
+        leaving_grad=images_low(),
+        spread_act=hold(images_here, padded, 3 * channels),
+        spread_two=hold(images_here, padded, 3 * channels),
+        spread_one=hold(images_here, padded, 3 * channels),
+        spread_far=hold(images_here, padded, 3 * half),
+        hidden=fields(),
+        middle=fields(),
+        delta=fields(),
+        grad_middle=fields(),
+        probs=hold(flat_rows, pixels, kind=full),
+        act_one=activations(),
+        act_two=activations(),
+        act_one_far=activations(),
+        act_two_far=activations(),
+        normed=activations(),
+        query=activations(),
+        key=activations(),
+        value=activations(),
+        mixed=activations(),
+        grad_mixed=activations(),
+        grad_query=activations(),
+        grad_key=activations(),
+        grad_value=activations(),
+        grad_one=activations(),
+        grad_two=activations(),
+        grad_one_far=hold(flat_rows, half),
+        grad_two_far=hold(flat_rows, half),
+        blocks_one=hold(ranks, 2, conv_rows, half),
+        blocks_two=hold(ranks, 2, conv_rows, half),
+        blocks_mix=hold(ranks, 2, mix_rows, channels),
+        land_one=hold(halvings - 1, conv_rows, half),
+        land_two=hold(halvings - 1, conv_rows, half),
+        land_mix=hold(halvings, mix_rows, channels),
+        kept_one=hold(halvings - 3, conv_rows, half),
+        kept_two=hold(halvings - 3, conv_rows, half),
+        kept_mix=hold(halvings - 1, mix_rows, channels),
+        sum_one=hold(2, conv_rows, half, kind=full),
+        sum_two=hold(2, conv_rows, half, kind=full),
+        fin_one=hold(2, conv_rows, half),
+        fin_two=hold(2, conv_rows, half),
+        last_one=hold(conv_rows, half),
+        last_two=hold(conv_rows, half),
+        share_mix=hold(mix_rows, channels, kind=full),
+        small_sum=hold(bits + 2, 16, channels, kind=full),
+        small_land=hold(bits + 1, 16, channels, kind=full),
+        slots=hold(devices * 16, lanes, kind=full),
+        product=hold(channels, channels, kind=full),
+        same_group=hold(half, half),
+        load_sem=semaphores(8),
+        swap_send=semaphores(4 * images_here),
+        swap_recv=semaphores(4 * images_here),
+        swap_own=semaphores(4 * images_here),
+        share_send=semaphores(4 * images_here + 2),
+        share_recv=semaphores(4 * images_here + 2),
+        small_send=semaphores(bits + 1),
+        small_recv=semaphores(bits + 1),
+        slots_send=semaphores(2),
+        slots_recv=semaphores(2),
+        reduce_send_one=semaphores(bits, parts),
+        reduce_recv_one=semaphores(bits, parts),
+        reduce_send_two=semaphores(bits, parts),
+        reduce_recv_two=semaphores(bits, parts),
+        reduce_send_mix=semaphores(bits + 1, 1),
+        reduce_recv_mix=semaphores(bits + 1, 1),
+    )
+
+    in_vmem = pl.BlockSpec(memory_space=pltpu.VMEM)
+    anywhere = pl.BlockSpec(memory_space=pl.ANY)
+    in_smem = pl.BlockSpec(memory_space=pltpu.SMEM)
+    arrays, in_specs = {}, []
+    for name, value in given.items():
+        if value.ndim == 1 and value.dtype == full:
+            value = value.reshape(1, channels)
+            in_specs.append(in_vmem)
+        else:
+            in_specs.append(in_smem if value.ndim == 1 else anywhere)
+        arrays[name] = value
+    names = tuple(arrays) + tuple(outputs) + tuple(scratch)
+    output, input_grad, flat, sums = pl.pallas_call(
+        functools.partial(fused_kernel, names, spans, ranks, table_rows),
+        out_shape=tuple(outputs.values()),
+        in_specs=in_specs,
+        out_specs=(anywhere, anywhere, in_vmem, in_vmem),
+        scratch_shapes=list(scratch.values()),
+        compiler_params=pltpu.CompilerParams(
+            collective_id=0, has_side_effects=True, vmem_limit_bytes=63 << 20
+        ),
+        name="block",
+    )(*arrays.values())
+
+    order = dict(table=0, conv_one=0, conv_two=0, embed=0, query=0, key=0, value=0, out=0)
+    sizes["table"] = table_rows * channels // devices // lanes
+    finals = [struct((sizes[name], lanes), full) for name in order]
+    rows = [SUMS.index(name) for name in GIVEN_BACK]
+    results = pl.pallas_call(
+        functools.partial(last_kernel, [spans[name] for name in order], rows),
+        out_shape=(outputs["output"], outputs["input_grad"], *finals)
+        + (struct((1, channels), full),) * len(rows),
+        in_specs=[anywhere, anywhere, anywhere, in_vmem],
+        out_specs=(anywhere,) * (2 + len(finals)) + (in_vmem,) * len(rows),
+        scratch_shapes=[
+            hold(*images.shape),
+            hold(*images.shape),
+            hold(start, lanes, kind=full),
+            semaphores(5 + len(finals)),
+        ],
+        compiler_params=pltpu.CompilerParams(vmem_limit_bytes=63 << 20),
+        name="finish",
+    )(output, input_grad, flat, sums)
+    return tuple(results[:2]) + tuple(member.reshape(-1) for member in results[2:])
+
+
+def per_device(
+    images,
+    cotangent,
+    levels,
+    noise_table,
+    gain_one,
+    shift_one,
+    conv_one,
+    bias_one,
+    embed_weight,
+    embed_bias,
+    gain_two,
+    shift_two,
+    conv_two,
+    bias_two,
+    gain_three,
+    shift_three,
+    query_weight,
+    query_bias,
+    key_weight,
+    value_weight,
+    value_bias,
+    out_weight,
+    out_bias,
+):
+    given = dict(
+        images=images,
+        cotangent=cotangent,
+        levels=levels,
+        noise_table=noise_table,
+        gain_one=gain_one,
+        shift_one=shift_one,
+        conv_one=conv_one,
+        bias_one=bias_one,
+        embed_weight=embed_weight,
+        embed_bias=embed_bias,
+        gain_two=gain_two,
+        shift_two=shift_two,
+        conv_two=conv_two,
+        bias_two=bias_two,
+        gain_three=gain_three,
+        shift_three=shift_three,
+        query_weight=query_weight,
+        query_bias=query_bias,
+        key_weight=key_weight,
+        value_weight=value_weight,
+        value_bias=value_bias,
+        out_weight=out_weight,
+        out_bias=out_bias,
+    )
+    ranks, cores = lax.axis_size("wide"), lax.axis_size("rep")
+    images_rep, piece, channels = images.shape
+    devices = ranks * cores
+    fits = (
+        cores == 2
+        and ranks >= 8
+        and ranks & (ranks - 1) == 0
+        and images_rep == 2 * ranks
+        and piece % 16 == 0
+        and conv_one.shape[0] % (devices * 48) == 0
+        and channels % (devices * 16) == 0
+        and noise_table.size % (devices * channels // 2) == 0
+    )
+    return fused_device(given) if fits else plain_device(*given.values())
+
+
 def solution(mesh):
     in_specs = (
         P("rep", "wide", None),

time: 741 us -> 111 us (0.15); the launches traced: 732 us -> 111 us
  waiting for transfers between devices: 402 us -> 0 us
  local copies, waits for them, and re-layouts: 126 us -> 0 us
  Pallas kernels: 0 us -> 110 us
  other arithmetic: 66.2 us -> 0 us
  matrix products: 55.6 us -> 0 us
  blocking collectives: 42.8 us -> 0 us
  starting transfers between devices: 23.1 us -> 0 us
  between operations: 15.5 us -> 0.84 us
    unnamed x2 -> x0, waiting for transfers between devices: 371 us -> none
    pallas_call x0 -> x2, Pallas kernels: none -> 110 us  [the longest x1 106 us: fused_device(): pl.pallas_call(functools.partial(fused_kernel, names, spans, ranks, table...]
    reshape x13 -> x0, local copies, waits for them, and re-layouts: 59.1 us -> none  [the longest x8 30.2 us: per_device(): member.reshape(device_count, -1)]
    dot_general x29 -> x0, matrix products: 55.6 us -> none  [the longest x6 21.3 us: contract_rows(): lax.dot_general(left, right, (((0,), (0,)), ((), ())), preferred_element_...]
    reduce_sum x22 -> x0, other arithmetic: 52.3 us -> none  [the longest x4 13.5 us: group_norm(): center = jnp.mean(grouped, axis=(1, 3), keepdims=True)]
    psum x1 -> x0, blocking collectives: 42.8 us -> none  [per_device(): lax.psum((grad_gain_one, grad_shift_one, grad_bias_one, grad_embed_bias,...]
    unnamed x140 -> x0, local copies, waits for them, and re-layouts: 32.2 us -> none
    all_to_all x4 -> x0, waiting for transfers between devices: 31.2 us -> none  [the longest x1 20.8 us: per_device(): lax.all_to_all(result.reshape(images_here, pixels, channels).astype(jnp.b...]
  transfers between devices with their start and end apart: 5 -> 0, of which waited for: 3 -> 0; matrix products, arithmetic and copies ran while one was open for 9% -> 0% of each run, Pallas kernels for 0% -> 0%
where the time goes in v2:
time: 111 us
  Pallas kernels  110 us (99%)
    pallas_call x1, Pallas kernels, fused_device(): pl.pallas_call(functools.partial(fused_kernel, names, spans, ranks, table...  106 us
    pallas_call x1, Pallas kernels, fused_device(): pl.pallas_call(functools.partial(last_kernel, [spans[name] for name in or...  3.9 us

profile of v2, /device:TPU:0, one launch (start us, length us, event | category | flops | bytes accessed | tf_op | source)
XLA Modules:
  0.0 110.6 jit_solution(4707308005214606065)
XLA Ops:
  0.7 105.9 %block.1 = (bf16[32,16,512]{2,1,0:T(8,128)(2,1)}, bf16[32,16,512]{2,1,0:T(8,128)(2,1)}, f32[1728,128]{1,0:T(8,128)}, f32[16,512]{1,0:T(8,128)}) custom-call(bf16[32,16,512]{2,1,0:T(8,128)(2,1)} %refs_0_.1, bf16[32,16,512]{2,1,0:T(8,128)(2,1)} %refs_1_.1, s32[32]{0:T(128)} %refs_2_.1, bf16[2000,512]{1,0:T(8,128)(2,1)} %refs_3_.1, f32[1,512]{1,0:T(1,128)} %bitcast.32, ...), custom_call_target="tpu_custom_call" | custom-call | tf_op jit(solution)/shard_map/block/pallas_call | solution.py:1426
  106.5 3.9 %finish.1 = (bf16[32,16,512]{2,1,0:T(8,128)(2,1)}, bf16[32,16,512]{2,1,0:T(8,128)(2,1)}, f32[250,128]{1,0:T(8,128)}, f32[576,128]{1,0:T(8,128)}, f32[576,128]{1,...) custom-call(bf16[32,16,512]{2,1,0:T(8,128)(2,1)} %get-tuple-element., ...), custom_call_target="tpu_custom_call" | custom-call | tf_op jit(solution)/shard_map/finish/pallas_call | solution.py:1442

commit v3 on v2

--- a/solution.py
+++ b/solution.py
@@ -358,9 +358,9 @@
 
 
 class Reduce:
-    def __init__(self, flights, place, blocks, bits, landing, kept, send, recv, last):
+    def __init__(self, flights, place, blocks, orders, landing, kept, send, recv, last):
         self.flights, self.place = flights, place
-        self.blocks, self.bits, self.last = blocks, bits, last
+        self.blocks, self.orders, self.last = blocks, orders, last
         self.landing, self.kept, self.send, self.recv = landing, kept, send, recv
         self.rows = blocks.shape[2]
         self.parts = send.shape[1]
@@ -377,7 +377,7 @@
             target = place.other_core
         else:
             count = self.blocks.shape[0] >> stage
-            bit = self.bits[stage - 1]
+            bit = self.orders[part][stage - 1]
             source = self.kept[stage - 1].at[
                 pl.ds((1 - place.bit(bit)) * count, count), rows, :
             ]
@@ -397,7 +397,7 @@
 
     def step(self, stage, part):
         self.finish(stage, part)
-        if stage < len(self.bits):
+        if stage < len(self.orders[part]):
             self.start(stage + 1, part)
 
     def finish(self, stage, part):
@@ -407,10 +407,10 @@
         if stage == 0:
             own = self.blocks[:, place.core, rows, :]
         else:
-            first = place.bit(self.bits[stage - 1]) * count
+            first = place.bit(self.orders[part][stage - 1]) * count
             own = self.kept[stage - 1][pl.ds(first, count), rows, :]
         landed = self.landing[stage][:, rows, :]
-        if stage < len(self.bits):
+        if stage < len(self.orders[part]):
             self.kept[stage][:, rows, :] = own + landed
         else:
             self.last(rows, own.astype(jnp.float32) + landed.astype(jnp.float32))
@@ -555,6 +555,8 @@
     swap_grad = swaps(scatter_copy, scatter_own, 3, s.leaving_grad, s.input_grad, s.leaving_grad)
     for image in every_image:
         swap_images[image].start()
+    for image in every_image:
+        swap_upstream[image].start()
 
     for padded in (s.spread_act, s.spread_two, s.spread_one, s.spread_far):
         for image in every_image:
@@ -565,6 +567,23 @@
     if tail:
         s.noise_table_here[table_rows:, :] = jnp.zeros((tail, channels), jnp.bfloat16)
     own_levels = [s.levels[place.rank * images_here + image] for image in every_image]
+    lane = lax.broadcasted_iota(jnp.int32, s.levels_all.shape[1:], 1)
+    tile = jnp.zeros(lane.shape, jnp.float32)
+    for index in range(ranks * images_here):
+        tile = jnp.where(lane == index, s.levels[index].astype(jnp.float32), tile)
+    s.levels_all[place.core] = tile
+
+    def levels_copy():
+        return pltpu.make_async_remote_copy(
+            src_ref=s.levels_all.at[place.core],
+            dst_ref=s.levels_all.at[place.core],
+            send_sem=s.slots_send.at[2],
+            recv_sem=s.slots_recv.at[2],
+            device_id=place.other_core,
+            device_id_type=MESH,
+        )
+
+    levels_pair = Flight(flights, levels_copy).start()
     entry = lax.broadcasted_iota(jnp.int32, (8, s.noise_table_here.shape[0]), 1)
     line = lax.broadcasted_iota(jnp.int32, entry.shape, 0)
     selected = jnp.zeros(entry.shape, jnp.float32)
@@ -715,6 +734,7 @@
         for image in every_image:
             over(image, unfold, 0)
         rows_block = blocks.shape[2]
+        rows_part = rows_block // len(spots)
         for tap in range(9):
             rows, side_tap = tap_rows(tap // 3), tap % 3
             near = spread[
@@ -728,18 +748,19 @@
             done = 0
             while done < channels:
                 block, inside = divmod(tap * channels + done, rows_block)
-                size = min(rows_block - inside, channels - done)
-                blocks[spots[block // 2], block % 2, inside : inside + size, :] = product[
+                part = inside // rows_part
+                size = min(rows_part * (part + 1) - inside, channels - done)
+                blocks[spots[part][block // 2], block % 2, inside : inside + size, :] = product[
                     done : done + size
                 ]
                 done = done + size
 
-    order_one = [1 - bit_one] + far
-    order_two = [1 - bit_two] + far
-    order_mix = [0, 1] + far
-    spots_one = block_order(ranks, order_one + [bit_one])
-    spots_two = block_order(ranks, order_two + [bit_two])
-    spots_mix = block_order(ranks, order_mix)
+    orders_one = [[1 - bit_one] + far] * 2 + [far + [1 - bit_one]]
+    orders_two = [[1 - bit_two] + far] * 2 + [far + [1 - bit_two]]
+    orders_mix = [[0, 1] + far, [1, 0] + far]
+    spots_one = [block_order(ranks, order + [bit_one]) for order in orders_one]
+    spots_two = [block_order(ranks, order + [bit_two]) for order in orders_two]
+    spots_mix = [block_order(ranks, order) for order in orders_mix]
 
     def put_one(rows, total):
         s.sum_one[:, rows, :] = total
@@ -760,7 +781,7 @@
         return views
 
     def reduction(blocks, order, landing, kept, send, recv, put):
-        stages = len(order)
+        stages = len(order[0])
         return Reduce(
             flights,
             place,
@@ -775,7 +796,7 @@
 
     reduce_one = reduction(
         s.blocks_one,
-        order_one,
+        orders_one,
         s.land_one,
         s.kept_one,
         s.reduce_send_one,
@@ -784,7 +805,7 @@
     )
     reduce_two = reduction(
         s.blocks_two,
-        order_two,
+        orders_two,
         s.land_two,
         s.kept_two,
         s.reduce_send_two,
@@ -793,7 +814,7 @@
     )
     reduce_mix = reduction(
         s.blocks_mix,
-        order_mix,
+        orders_mix,
         s.land_mix,
         s.kept_mix,
         s.reduce_send_mix,
@@ -828,7 +849,7 @@
         if stage < bits:
             small[stage + 1].start()
 
-    slot_rows = 16
+    slot_rows = 8
     lanes = s.slots.shape[1]
 
     def pair_window():
@@ -897,9 +918,6 @@
     def forward(image):
         rows = image_rows(image)
         swap_images[image].arrive()
-        if image == images_here - 1:
-            for later in every_image:
-                swap_upstream[later].start()
         moments_one.append(statistics(load_input, image))
         activate(load_input, image, moments_one[image], gain_one, shift_one, s.act_one)
         share_act_one[image].start()
@@ -971,6 +989,8 @@
             + against(grad_value, s.value_weight_here[...])
         )
 
+    def backward_rest(image, between=None):
+        rows = image_rows(image)
         center, rate = moments_three[image]
 
         def sums_three(image, step, totals):
@@ -996,6 +1016,8 @@
 
         sums["bias_two"].append(whole(over(image, back_three, none)))
         share_grad_two[image].start()
+        if between is not None:
+            between()
 
         s.delta[rows, :] = convolve_back(s.spread_two, s.conv_two_here, slice(image, image + 1))
 
@@ -1036,6 +1058,9 @@
         return gain_sum, shift_sum, over(image, back, start)
 
     def backward_input(image):
+        s.delta[image_rows(image), :] = convolve_back(
+            s.spread_one, s.conv_one_here, slice(image, image + 1)
+        )
         def put_input(image, step, grad, carry):
             total = grad + s.grad_middle[flat_at(image, step), :]
             s.leaving_grad[image, at(step), :] = total.astype(jnp.bfloat16)
@@ -1055,9 +1080,10 @@
         for rank in range(ranks):
             for core in range(2):
                 block = rank * 2 + core
-                s.blocks_mix[
-                    spots_mix[rank], core, which * mix_rows : (which + 1) * mix_rows, :
-                ] = product[block * mix_rows : (block + 1) * mix_rows]
+                spot = spots_mix[which // 2][rank]
+                s.blocks_mix[spot, core, which * mix_rows : (which + 1) * mix_rows, :] = product[
+                    block * mix_rows : (block + 1) * mix_rows
+                ]
 
     def weigh_mix():
         upstream = s.upstream[...].reshape(flat_rows, channels)
@@ -1087,11 +1113,6 @@
                     jnp.broadcast_to(row, slot.shape),
                     slot,
                 )
-            slot = jnp.where(
-                slot_place == images_here * per_image + image,
-                own_levels[image].astype(jnp.float32),
-                slot,
-            )
         device = place.rank * 2 + place.core
         s.slots[pl.ds(pl.multiple_of(device * slot_rows, slot_rows), slot_rows), :] = slot
 
@@ -1116,9 +1137,13 @@
             ],
             axis=0,
         )
-        levels = jnp.concatenate(
-            [every(images_here * per_image + image) for image in every_image], axis=0
-        ).astype(jnp.int32)[:, 0:1]
+        place_of = lax.broadcasted_iota(jnp.int32, (images_here * ranks * 2, lanes), 0)
+        lane = lax.broadcasted_iota(jnp.int32, place_of.shape, 1)
+        wanted = (place_of % (ranks * 2)) // 2 * images_here + place_of // (ranks * 2)
+        tiles = [jnp.broadcast_to(s.levels_all[core, 0:1, :], place_of.shape) for core in (0, 1)]
+        chosen = jnp.where(place_of % 2 == 0, tiles[0], tiles[1])
+        levels = jnp.sum(jnp.where(lane == wanted, chosen, 0.0), axis=1, keepdims=True)
+        levels = levels.astype(jnp.int32)
         entry = lax.broadcasted_iota(
             jnp.int32, (levels.shape[0], s.noise_table_here.shape[0]), 1
         )
@@ -1146,10 +1171,12 @@
             )
         flat(spans["table"], total)
 
-    def start_small():
+    def sum_biases():
         sums["query_bias"].append(column_sums(load_low(s.grad_query)))
         sums["value_bias"].append(column_sums(load_low(s.grad_value)))
         sums["out_bias"].append(column_sums(load_upstream))
+
+    def start_small():
         rows = [functools.reduce(jnp.add, sums[name]) for name in SUMS]
         s.small_sum[0, 0:8, :] = stack_rows(rows[:8])
         s.small_sum[0, 8:16, :] = stack_rows(rows[8:])
@@ -1161,15 +1188,21 @@
 
     for image in every_image:
         forward(image)
-    backward(0)
-    for image in every_image[1:]:
-        backward(image)
     for image in every_image:
         swap_output[image].start()
+    for image in every_image[:-1]:
+        backward(image)
+        backward_rest(image)
+        backward_input(image)
+    backward(images_here - 1)
+    backward_rest(images_here - 1)
     fill_slot()
     slots_pair.start()
     weigh_mix()
     reduce_mix.start(0, 0)
+    reduce_mix.start(0, 1)
+    backward_input(images_here - 1)
+    step_all(reduce_mix, 0)
     slots_pair.arrive()
     slots_all.start()
     for image in every_image:
@@ -1180,12 +1213,6 @@
     )
     for part in range(parts):
         reduce_two.start(0, part)
-    reduce_mix.step(0, 0)
-    s.delta[...] = convolve_back(s.spread_one, s.conv_one_here, slice(None))
-    for image in every_image:
-        backward_input(image)
-    start_small()
-    step_all(reduce_two, 0)
     for image in every_image:
         share_act_one[image].arrive()
         share_grad_one[image].arrive()
@@ -1194,44 +1221,51 @@
     )
     for part in range(parts):
         reduce_one.start(0, part)
-    small_step(0)
+    step_all(reduce_two, 0)
+    sum_biases()
+    start_small()
     step_all(reduce_one, 0)
-    slots_all.arrive()
-    embedding_gradients()
+    reduce_two.step(1, 0)
+    reduce_two.step(1, 2)
+    reduce_one.step(1, 2)
+    reduce_mix.step(1, 1)
     reduce_mix.step(1, 0)
-    small_step(1)
-
-    reduce_two.step(1, 0)
     reduce_one.step(1, 0)
     reduce_two.step(1, 1)
     reduce_two.step(2, 0)
-    reduce_mix.step(2, 0)
-    small_step(2)
+    reduce_two.step(2, 2)
+    small_step(0)
+    reduce_one.step(2, 2)
     reduce_one.step(1, 1)
     reduce_one.step(2, 0)
-    reduce_two.step(1, 2)
     reduce_two.step(2, 1)
+    reduce_mix.step(2, 1)
+    reduce_mix.step(2, 0)
+    small_step(1)
     reduce_two.step(3, 0)
+    reduce_two.step(3, 2)
+    levels_pair.arrive()
+    slots_all.arrive()
+    embedding_gradients()
+    reduce_one.step(3, 0)
+    reduce_one.step(3, 2)
+    small_step(2)
+    reduce_mix.step(3, 1)
     reduce_mix.step(3, 0)
+    reduce_one.step(2, 1)
+    reduce_two.step(3, 1)
+    end_two = share_copy(4 * images_here, s.fin_two.at[1 - half_two], s.last_two, bit_two).start()
     small_step(3)
-    reduce_one.step(1, 2)
-    reduce_one.step(2, 1)
-    reduce_one.step(3, 0)
-    reduce_two.step(2, 2)
-    reduce_two.step(3, 1)
-    reduce_mix.step(4, 0)
-    small_step(4)
-    s.sums[...] = s.small_sum[bits + 1]
-    for index, name in enumerate(dict(query=0, key=0, value=0, out=0)):
-        flat(spans[name], s.share_mix[index * mix_rows : (index + 1) * mix_rows, :])
-    reduce_one.step(2, 2)
     reduce_one.step(3, 1)
-    reduce_two.step(3, 2)
-    end_two = share_copy(4 * images_here, s.fin_two.at[1 - half_two], s.last_two, bit_two).start()
-    reduce_one.step(3, 2)
     end_one = share_copy(
         4 * images_here + 1, s.fin_one.at[1 - half_one], s.last_one, bit_one
     ).start()
+    reduce_mix.step(4, 1)
+    reduce_mix.step(4, 0)
+    for index, name in enumerate(dict(query=0, key=0, value=0, out=0)):
+        flat(spans[name], s.share_mix[index * mix_rows : (index + 1) * mix_rows, :])
+    small_step(4)
+    s.sums[...] = s.small_sum[bits + 1]
     flat(spans["conv_two"], settle(end_two, s.sum_two, s.last_two, half_two))
     flat(spans["conv_one"], settle(end_one, s.sum_one, s.last_one, half_one))
 
@@ -1390,7 +1424,8 @@
         share_mix=hold(mix_rows, channels, kind=full),
         small_sum=hold(bits + 2, 16, channels, kind=full),
         small_land=hold(bits + 1, 16, channels, kind=full),
-        slots=hold(devices * 16, lanes, kind=full),
+        slots=hold(devices * 8, lanes, kind=full),
+        levels_all=hold(2, 8, lanes, kind=full),
         product=hold(channels, channels, kind=full),
         same_group=hold(half, half),
         load_sem=semaphores(8),
@@ -1401,14 +1436,14 @@
         share_recv=semaphores(4 * images_here + 2),
         small_send=semaphores(bits + 1),
         small_recv=semaphores(bits + 1),
-        slots_send=semaphores(2),
-        slots_recv=semaphores(2),
+        slots_send=semaphores(3),
+        slots_recv=semaphores(3),
         reduce_send_one=semaphores(bits, parts),
         reduce_recv_one=semaphores(bits, parts),
         reduce_send_two=semaphores(bits, parts),
         reduce_recv_two=semaphores(bits, parts),
-        reduce_send_mix=semaphores(bits + 1, 1),
-        reduce_recv_mix=semaphores(bits + 1, 1),
+        reduce_send_mix=semaphores(bits + 1, 2),
+        reduce_recv_mix=semaphores(bits + 1, 2),
     )
 
     in_vmem = pl.BlockSpec(memory_space=pltpu.VMEM)

time: 111 us -> 104 us (0.937)
  Pallas kernels: 110 us -> 103 us
    pallas_call x1, Pallas kernels: 106 us -> 98.9 us  [fused_device(): pl.pallas_call(functools.partial(fused_kernel, names, spans, ranks, table...]
where the time goes in v3:
time: 104 us
  Pallas kernels  103 us (99%)
    pallas_call x1, Pallas kernels, fused_device(): pl.pallas_call(functools.partial(fused_kernel, names, spans, ranks, table...  98.9 us
    pallas_call x1, Pallas kernels, fused_device(): pl.pallas_call(functools.partial(last_kernel, [spans[name] for name in or...  3.9 us

profile of v3, /device:TPU:0, one launch (start us, length us, event | category | flops | bytes accessed | tf_op | source)
XLA Modules:
  0.0 103.7 jit_solution(17961777690646075423)
XLA Ops:
  0.7 98.9 %block.1 = (bf16[32,16,512]{2,1,0:T(8,128)(2,1)}, bf16[32,16,512]{2,1,0:T(8,128)(2,1)}, f32[1728,128]{1,0:T(8,128)}, f32[16,512]{1,0:T(8,128)}) custom-call(bf16[32,16,512]{2,1,0:T(8,128)(2,1)} %refs_0_.1, bf16[32,16,512]{2,1,0:T(8,128)(2,1)} %refs_1_.1, s32[32]{0:T(128)} %refs_2_.1, bf16[2000,512]{1,0:T(8,128)(2,1)} %refs_3_.1, f32[1,512]{1,0:T(1,128)} %bitcast.32, ...), custom_call_target="tpu_custom_call" | custom-call | tf_op jit(solution)/shard_map/block/pallas_call | solution.py:1461
  99.6 3.9 %finish.1 = (bf16[32,16,512]{2,1,0:T(8,128)(2,1)}, bf16[32,16,512]{2,1,0:T(8,128)(2,1)}, f32[250,128]{1,0:T(8,128)}, f32[576,128]{1,0:T(8,128)}, f32[576,128]{1,...) custom-call(bf16[32,16,512]{2,1,0:T(8,128)(2,1)} %get-tuple-element., ...), custom_call_target="tpu_custom_call" | custom-call | tf_op jit(solution)/shard_map/finish/pallas_call | solution.py:1477

commit v4 on v3

--- a/solution.py
+++ b/solution.py
@@ -358,10 +358,11 @@
 
 
 class Reduce:
-    def __init__(self, flights, place, blocks, orders, landing, kept, send, recv, last):
+    def __init__(self, flights, place, blocks, orders, landing, kept, send, recv, last, spread):
         self.flights, self.place = flights, place
         self.blocks, self.orders, self.last = blocks, orders, last
         self.landing, self.kept, self.send, self.recv = landing, kept, send, recv
+        self.spread, self.stages = spread, max(len(order) for order in orders)
         self.rows = blocks.shape[2]
         self.parts = send.shape[1]
         self.under_way = {}
@@ -399,6 +400,8 @@
         self.finish(stage, part)
         if stage < len(self.orders[part]):
             self.start(stage + 1, part)
+        elif stage < self.stages:
+            self.spread(self.kept[stage], self.cut(part))
 
     def finish(self, stage, part):
         place, rows = self.place, self.cut(part)
@@ -410,7 +413,7 @@
             first = place.bit(self.orders[part][stage - 1]) * count
             own = self.kept[stage - 1][pl.ds(first, count), rows, :]
         landed = self.landing[stage][:, rows, :]
-        if stage < len(self.orders[part]):
+        if stage < self.stages:
             self.kept[stage][:, rows, :] = own + landed
         else:
             self.last(rows, own.astype(jnp.float32) + landed.astype(jnp.float32))
@@ -755,11 +758,16 @@
                 ]
                 done = done + size
 
-    orders_one = [[1 - bit_one] + far] * 2 + [far + [1 - bit_one]]
-    orders_two = [[1 - bit_two] + far] * 2 + [far + [1 - bit_two]]
+    orders_one = [[1 - bit_one] + far, far + [1 - bit_one], [1 - bit_one]]
+    orders_two = [[1 - bit_two] + far, far + [1 - bit_two], [1 - bit_two]]
     orders_mix = [[0, 1] + far, [1, 0] + far]
-    spots_one = [block_order(ranks, order + [bit_one]) for order in orders_one]
-    spots_two = [block_order(ranks, order + [bit_two]) for order in orders_two]
+    tails_one, tails_two = ([bit_one],) * 2 + (far + [bit_one],), ([bit_two],) * 2 + (far + [bit_two],)
+    spots_one = [
+        block_order(ranks, order + end) for order, end in zip(orders_one, tails_one, strict=True)
+    ]
+    spots_two = [
+        block_order(ranks, order + end) for order, end in zip(orders_two, tails_two, strict=True)
+    ]
     spots_mix = [block_order(ranks, order) for order in orders_mix]
 
     def put_one(rows, total):
@@ -772,6 +780,58 @@
 
     def put_mix(rows, total):
         s.share_mix[rows, :] = total[0]
+
+    owners = ranks // 2
+
+    def straight(slot, bit, land):
+        order = far + [bit]
+        weights = [1 << (len(order) - 1 - k) for k in range(len(order))]
+        own = sum(place.bit(b) * weight for b, weight in zip(order, weights, strict=True))
+        other = 1 - bit
+
+        def send(kept, rows):
+            land[own] = kept[own, rows, :]
+
+            def make(offset):
+                target = (own + offset) % owners
+                rank = place.bit(other) * (1 << other)
+                for b, weight in zip(order, weights, strict=True):
+                    rank = rank + (target // weight) % 2 * (1 << b)
+                return pltpu.make_async_remote_copy(
+                    src_ref=kept.at[target, rows, :],
+                    dst_ref=land.at[own],
+                    send_sem=s.straight_send.at[slot],
+                    recv_sem=s.straight_recv.at[slot],
+                    device_id=(rank, place.core),
+                    device_id_type=MESH,
+                )
+
+            def everything():
+                others = land.at[pl.ds(0, owners - 1)]
+                return pltpu.make_async_remote_copy(
+                    src_ref=others,
+                    dst_ref=others,
+                    send_sem=s.straight_send.at[slot],
+                    recv_sem=s.straight_recv.at[slot],
+                    device_id=place.across(0),
+                    device_id_type=MESH,
+                )
+
+            flight_to[slot] = Flight(flights, make, (1, owners), everything).start()
+
+        return send
+
+    flight_to = {}
+
+    def gather_straight(slot, land):
+        flight_to[slot].arrive()
+        sides = []
+        for side in (0, 1):
+            total = land[side].astype(jnp.float32)
+            for index in range(side + 2, owners, 2):
+                total = total + land[index].astype(jnp.float32)
+            sides.append(total)
+        return jnp.concatenate(sides, axis=1)
 
     def staged(ref, first, stages):
         views, start = [], 0
@@ -780,7 +840,7 @@
             start = start + (first >> stage)
         return views
 
-    def reduction(blocks, order, landing, kept, send, recv, put):
+    def reduction(blocks, order, landing, kept, send, recv, put, spread=None):
         stages = len(order[0])
         return Reduce(
             flights,
@@ -792,6 +852,7 @@
             send,
             recv,
             put,
+            spread,
         )
 
     reduce_one = reduction(
@@ -802,6 +863,7 @@
         s.reduce_send_one,
         s.reduce_recv_one,
         put_one,
+        straight(0, bit_one, s.straight_one),
     )
     reduce_two = reduction(
         s.blocks_two,
@@ -811,6 +873,7 @@
         s.reduce_send_two,
         s.reduce_recv_two,
         put_two,
+        straight(1, bit_two, s.straight_two),
     )
     reduce_mix = reduction(
         s.blocks_mix,
@@ -822,10 +885,12 @@
         put_mix,
     )
     parts = reduce_one.parts
+    chain_rows = s.last_one.shape[0]
+    chain = pl.ds(0, chain_rows)
 
     def settle(flight, sums, target, mine):
         flight.arrive()
-        own = sums[mine]
+        own = sums[mine, 0:chain_rows, :]
         other = target[...].astype(jnp.float32)
         left = jnp.where(mine == 0, own, other)
         right = jnp.where(mine == 0, other, own)
@@ -1188,12 +1253,12 @@
 
     for image in every_image:
         forward(image)
-    for image in every_image:
-        swap_output[image].start()
     for image in every_image[:-1]:
         backward(image)
         backward_rest(image)
         backward_input(image)
+    for image in every_image:
+        swap_output[image].start()
     backward(images_here - 1)
     backward_rest(images_here - 1)
     fill_slot()
@@ -1226,48 +1291,46 @@
     start_small()
     step_all(reduce_one, 0)
     reduce_two.step(1, 0)
-    reduce_two.step(1, 2)
-    reduce_one.step(1, 2)
+    reduce_two.step(1, 1)
     reduce_mix.step(1, 1)
     reduce_mix.step(1, 0)
+    reduce_one.step(1, 1)
     reduce_one.step(1, 0)
-    reduce_two.step(1, 1)
+    reduce_two.step(1, 2)
     reduce_two.step(2, 0)
-    reduce_two.step(2, 2)
+    reduce_two.step(2, 1)
     small_step(0)
-    reduce_one.step(2, 2)
-    reduce_one.step(1, 1)
-    reduce_one.step(2, 0)
-    reduce_two.step(2, 1)
-    reduce_mix.step(2, 1)
-    reduce_mix.step(2, 0)
-    small_step(1)
-    reduce_two.step(3, 0)
-    reduce_two.step(3, 2)
     levels_pair.arrive()
     slots_all.arrive()
     embedding_gradients()
+    reduce_one.step(2, 1)
+    reduce_one.step(2, 0)
+    reduce_one.step(1, 2)
+    reduce_two.step(3, 0)
+    reduce_two.step(3, 1)
+    end_two = share_copy(4 * images_here, s.fin_two.at[1 - half_two, chain], s.last_two, bit_two).start()
+    small_step(1)
+    reduce_mix.step(2, 1)
+    reduce_mix.step(2, 0)
     reduce_one.step(3, 0)
-    reduce_one.step(3, 2)
+    reduce_one.step(3, 1)
+    end_one = share_copy(
+        4 * images_here + 1, s.fin_one.at[1 - half_one, chain], s.last_one, bit_one
+    ).start()
     small_step(2)
     reduce_mix.step(3, 1)
     reduce_mix.step(3, 0)
-    reduce_one.step(2, 1)
-    reduce_two.step(3, 1)
-    end_two = share_copy(4 * images_here, s.fin_two.at[1 - half_two], s.last_two, bit_two).start()
     small_step(3)
-    reduce_one.step(3, 1)
-    end_one = share_copy(
-        4 * images_here + 1, s.fin_one.at[1 - half_one], s.last_one, bit_one
-    ).start()
     reduce_mix.step(4, 1)
     reduce_mix.step(4, 0)
     for index, name in enumerate(dict(query=0, key=0, value=0, out=0)):
         flat(spans[name], s.share_mix[index * mix_rows : (index + 1) * mix_rows, :])
+    flat(spans["conv_two"] + chain_rows * per_image, gather_straight(1, s.straight_two))
+    flat(spans["conv_two"], settle(end_two, s.sum_two, s.last_two, half_two))
+    flat(spans["conv_one"] + chain_rows * per_image, gather_straight(0, s.straight_one))
+    flat(spans["conv_one"], settle(end_one, s.sum_one, s.last_one, half_one))
     small_step(4)
     s.sums[...] = s.small_sum[bits + 1]
-    flat(spans["conv_two"], settle(end_two, s.sum_two, s.last_two, half_two))
-    flat(spans["conv_one"], settle(end_one, s.sum_one, s.last_one, half_one))
 
     for flight in flights:
         flight.land()
@@ -1419,8 +1482,12 @@
         sum_two=hold(2, conv_rows, half, kind=full),
         fin_one=hold(2, conv_rows, half),
         fin_two=hold(2, conv_rows, half),
-        last_one=hold(conv_rows, half),
-        last_two=hold(conv_rows, half),
+        last_one=hold(conv_rows // parts * (parts - 1), half),
+        last_two=hold(conv_rows // parts * (parts - 1), half),
+        straight_one=hold(ranks // 2, conv_rows // parts, half),
+        straight_two=hold(ranks // 2, conv_rows // parts, half),
+        straight_send=semaphores(2),
+        straight_recv=semaphores(2),
         share_mix=hold(mix_rows, channels, kind=full),
         small_sum=hold(bits + 2, 16, channels, kind=full),
         small_land=hold(bits + 1, 16, channels, kind=full),

time: 104 us -> 100 us (0.962)
  Pallas kernels: 103 us -> 98.2 us
    pallas_call x1, Pallas kernels: 98.9 us -> 94.3 us  [fused_device(): pl.pallas_call(functools.partial(fused_kernel, names, spans, ranks, table...]
where the time goes in v4:
time: 100 us; the launch traced here: 99.1 us
  Pallas kernels  98.2 us (98%)
    pallas_call x1, Pallas kernels, fused_device(): pl.pallas_call(functools.partial(fused_kernel, names, spans, ranks, table...  94.3 us
    pallas_call x1, Pallas kernels, fused_device(): pl.pallas_call(functools.partial(last_kernel, [spans[name] for name in or...  3.9 us

profile of v4, /device:TPU:0, one launch (start us, length us, event | category | flops | bytes accessed | tf_op | source)
XLA Modules:
  0.0 99.1 jit_solution(11635504177599567575)
XLA Ops:
  0.7 94.3 %block.1 = (bf16[32,16,512]{2,1,0:T(8,128)(2,1)}, bf16[32,16,512]{2,1,0:T(8,128)(2,1)}, f32[1728,128]{1,0:T(8,128)}, f32[16,512]{1,0:T(8,128)}) custom-call(bf16[32,16,512]{2,1,0:T(8,128)(2,1)} %refs_0_.1, bf16[32,16,512]{2,1,0:T(8,128)(2,1)} %refs_1_.1, s32[32]{0:T(128)} %refs_2_.1, bf16[2000,512]{1,0:T(8,128)(2,1)} %refs_3_.1, f32[1,512]{1,0:T(1,128)} %bitcast.32, ...), custom_call_target="tpu_custom_call" | custom-call | tf_op jit(solution)/shard_map/block/pallas_call | solution.py:1528
  95.0 3.9 %finish.1 = (bf16[32,16,512]{2,1,0:T(8,128)(2,1)}, bf16[32,16,512]{2,1,0:T(8,128)(2,1)}, f32[250,128]{1,0:T(8,128)}, f32[576,128]{1,0:T(8,128)}, f32[576,128]{1,...) custom-call(bf16[32,16,512]{2,1,0:T(8,128)(2,1)} %get-tuple-element., ...), custom_call_target="tpu_custom_call" | custom-call | tf_op jit(solution)/shard_map/finish/pallas_call | solution.py:1544

commit v5 on v4

--- a/solution.py
+++ b/solution.py
@@ -758,8 +758,8 @@
                 ]
                 done = done + size
 
-    orders_one = [[1 - bit_one] + far, far + [1 - bit_one], [1 - bit_one]]
-    orders_two = [[1 - bit_two] + far, far + [1 - bit_two], [1 - bit_two]]
+    orders_one = [[1 - bit_one] + far] * 2 + [[1 - bit_one]]
+    orders_two = [[1 - bit_two] + far] * 2 + [[1 - bit_two]]
     orders_mix = [[0, 1] + far, [1, 0] + far]
     tails_one, tails_two = ([bit_one],) * 2 + (far + [bit_one],), ([bit_two],) * 2 + (far + [bit_two],)
     spots_one = [
@@ -1287,32 +1287,32 @@
     for part in range(parts):
         reduce_one.start(0, part)
     step_all(reduce_two, 0)
+    step_all(reduce_one, 0)
     sum_biases()
     start_small()
-    step_all(reduce_one, 0)
     reduce_two.step(1, 0)
+    reduce_one.step(1, 0)
     reduce_two.step(1, 1)
+    reduce_two.step(2, 0)
     reduce_mix.step(1, 1)
     reduce_mix.step(1, 0)
     reduce_one.step(1, 1)
-    reduce_one.step(1, 0)
+    reduce_one.step(2, 0)
     reduce_two.step(1, 2)
-    reduce_two.step(2, 0)
     reduce_two.step(2, 1)
     small_step(0)
+    reduce_one.step(2, 1)
+    reduce_two.step(3, 0)
+    reduce_one.step(1, 2)
     levels_pair.arrive()
     slots_all.arrive()
     embedding_gradients()
-    reduce_one.step(2, 1)
-    reduce_one.step(2, 0)
-    reduce_one.step(1, 2)
-    reduce_two.step(3, 0)
+    reduce_one.step(3, 0)
     reduce_two.step(3, 1)
     end_two = share_copy(4 * images_here, s.fin_two.at[1 - half_two, chain], s.last_two, bit_two).start()
     small_step(1)
     reduce_mix.step(2, 1)
     reduce_mix.step(2, 0)
-    reduce_one.step(3, 0)
     reduce_one.step(3, 1)
     end_one = share_copy(
         4 * images_here + 1, s.fin_one.at[1 - half_one, chain], s.last_one, bit_one
@@ -1330,7 +1330,8 @@
     flat(spans["conv_one"] + chain_rows * per_image, gather_straight(0, s.straight_one))
     flat(spans["conv_one"], settle(end_one, s.sum_one, s.last_one, half_one))
     small_step(4)
-    s.sums[...] = s.small_sum[bits + 1]
+    for index in range(len(SUMS)):
+        s.sums[index] = s.small_sum[bits + 1, index : index + 1, :]
 
     for flight in flights:
         flight.land()
@@ -1338,28 +1339,31 @@
 
 def last_kernel(starts, rows, *refs):
     output_in, grad_in, flat_in, sums_in, output, grad = refs[:6]
-    flats, sums = refs[6 : 6 + len(starts)], refs[6 + len(starts) : -4]
-    output_here, grad_here, flat_here, sems = refs[-4:]
+    flats, sums = refs[6 : 6 + len(starts)], refs[6 + len(starts) : -5]
+    output_here, grad_here, flat_here, sums_here, sems = refs[-5:]
     arrive = [
-        pltpu.make_async_copy(output_in, output_here, sems.at[0]),
-        pltpu.make_async_copy(grad_in, grad_here, sems.at[1]),
-        pltpu.make_async_copy(flat_in, flat_here, sems.at[2]),
+        pltpu.make_async_copy(sums_in, sums_here, sems.at[0]),
+        pltpu.make_async_copy(output_in, output_here, sems.at[1]),
+        pltpu.make_async_copy(grad_in, grad_here, sems.at[2]),
+        pltpu.make_async_copy(flat_in, flat_here, sems.at[3]),
     ]
     for move in arrive:
         move.start()
-    for row, target in zip(rows, sums, strict=True):
-        target[...] = sums_in[row : row + 1, :]
-    leave = [
-        pltpu.make_async_copy(output_here, output, sems.at[3]),
-        pltpu.make_async_copy(grad_here, grad, sems.at[4]),
+    ways = [
+        [(sums_here.at[row], target) for row, target in zip(rows, sums, strict=True)],
+        [(output_here, output)],
+        [(grad_here, grad)],
+        [
+            (flat_here.at[pl.ds(start, target.shape[0]), :], target)
+            for start, target in zip(starts, flats, strict=True)
+        ],
     ]
-    for index, (start, target) in enumerate(zip(starts, flats, strict=True)):
-        span = flat_here.at[pl.ds(start, target.shape[0]), :]
-        leave.append(pltpu.make_async_copy(span, target, sems.at[5 + index]))
-    for index, move in enumerate(arrive):
+    leave = []
+    for move, pairs in zip(arrive, ways, strict=True):
         move.wait()
-        for out in leave[index : index + 1] if index < 2 else leave[2:]:
-            out.start()
+        for source, target in pairs:
+            leave.append(pltpu.make_async_copy(source, target, sems.at[4 + len(leave)]))
+            leave[-1].start()
     for move in leave:
         move.wait()
 
@@ -1426,7 +1430,7 @@
         output=struct(images.shape, low),
         input_grad=struct(images.shape, low),
         flat=struct((start, lanes), full),
-        sums=struct((16, channels), full),
+        sums=struct((len(SUMS), 1, channels), full),
     )
     padded = pixels + 2 * SIDE
     halvings = sum(ranks >> stage for stage in range(bits + 1))
@@ -1545,13 +1549,14 @@
         functools.partial(last_kernel, [spans[name] for name in order], rows),
         out_shape=(outputs["output"], outputs["input_grad"], *finals)
         + (struct((1, channels), full),) * len(rows),
-        in_specs=[anywhere, anywhere, anywhere, in_vmem],
-        out_specs=(anywhere,) * (2 + len(finals)) + (in_vmem,) * len(rows),
+        in_specs=[anywhere] * 4,
+        out_specs=(anywhere,) * (2 + len(finals) + len(rows)),
         scratch_shapes=[
             hold(*images.shape),
             hold(*images.shape),
             hold(start, lanes, kind=full),
-            semaphores(5 + len(finals)),
+            hold(*outputs["sums"].shape, kind=full),
+            semaphores(6 + len(finals) + len(rows)),
         ],
         compiler_params=pltpu.CompilerParams(vmem_limit_bytes=63 << 20),
         name="finish",

time: 100 us -> 98.7 us (0.987)
    pallas_call x1, Pallas kernels: 3.9 us -> 2.64 us  [fused_device(): pl.pallas_call(functools.partial(last_kernel, [spans[name] for name in or...]
where the time goes in v5:
time: 98.7 us; the launch traced here: 98.5 us
  Pallas kernels  97.7 us (99%)
    pallas_call x1, Pallas kernels, fused_device(): pl.pallas_call(functools.partial(fused_kernel, names, spans, ranks, table...  95.1 us
    pallas_call x1, Pallas kernels, fused_device(): pl.pallas_call(functools.partial(last_kernel, [spans[name] for name in or...  2.64 us

profile of v5, /device:TPU:0, one launch (start us, length us, event | category | flops | bytes accessed | tf_op | source)
XLA Modules:
  0.0 98.5 jit_solution(14408739982131252659)
XLA Ops:
  0.7 95.1 %block.1 = (bf16[32,16,512]{2,1,0:T(8,128)(2,1)}, bf16[32,16,512]{2,1,0:T(8,128)(2,1)}, f32[1728,128]{1,0:T(8,128)}, f32[11,1,512]{2,1,0:T(1,128)}) custom-call(bf16[32,16,512]{2,1,0:T(8,128)(2,1)} %refs_0_.1, bf16[32,16,512]{2,1,0:T(8,128)(2,1)} %refs_1_.1, s32[32]{0:T(128)} %refs_2_.1, bf16[2000,512]{1,0:T(8,128)(2,1)} %refs_3_.1, f32[1,512]{1,0:T(1,128)} %bitcast.32, ...), custom_call_target="tpu_custom_call" | custom-call | tf_op jit(solution)/shard_map/block/pallas_call | solution.py:1532
  95.7 2.6 %finish.1 = (bf16[32,16,512]{2,1,0:T(8,128)(2,1)}, bf16[32,16,512]{2,1,0:T(8,128)(2,1)}, f32[250,128]{1,0:T(8,128)}, f32[576,128]{1,0:T(8,128)}, f32[576,128]{1,...) custom-call(bf16[32,16,512]{2,1,0:T(8,128)(2,1)} %get-tuple-element., ...), custom_call_target="tpu_custom_call" | custom-call | tf_op jit(solution)/shard_map/finish/pallas_call | solution.py:1548
